TPU v7x, 128 devices: a whole 4x4x4 slice. The times are simulated.
128 devices in a mesh: row: 8 (over y, core), col: 16 (over z, x).
Axes of the slice: x: 4, y: 4, z: 4, core: 2. Of those that a mesh axis runs over, the one named last changes fastest.
Arguments:
- factor: float32 [8, 8, 256, 4, 16, 256], P(None, 'row', None, None, 'col'), as said below
- adjoint: float32 [8, 8, 256, 4, 16, 256], P(None, 'row', None, None, 'col'), may hold values from -6 to 6
Outputs:
- adjoint_out: float32 [8, 8, 256, 4, 16, 256], P(None, 'row', None, None, 'col')
Inputs may be any that keep to these rules, and one draw needn't show every extreme that they name: factor is lower triangular with diagonal entries between 1 and 2.
All inputs are finite; a program needn't handle non-finite values.
Results may differ from a plain program's by a relative error of at most 0.00011.
Values sent between devices are 32-bit elements; how exact they have to be, the bound alone decides.
A program may use at most 192 MiB of HBM per device.

v0:
```python
import jax
import jax.numpy as jnp
from jax import lax
from jax.sharding import PartitionSpec as P

precise = lax.Precision.HIGHEST


def broadcast(block, axis, owner):
    block = jnp.where(lax.axis_index(axis) == owner, block, jnp.zeros_like(block))
    return lax.psum(block, axis)


def halve_diag(matrix):
    extent = matrix.shape[0]
    keep_mask = jnp.tril(jnp.ones((extent, extent), jnp.float32)) - 0.5 * jnp.eye(
        extent, dtype=jnp.float32
    )
    return matrix * keep_mask


def cholesky_adjoint(pivot_block, target_adjoint):
    inner_part = halve_diag(
        jnp.dot(
            pivot_block.T, target_adjoint, precision=precise, preferred_element_type=jnp.float32
        )
    )
    left_side = jax.scipy.linalg.solve_triangular(pivot_block, inner_part, trans=1, lower=True)
    both_sides = jax.scipy.linalg.solve_triangular(pivot_block, left_side.T, trans=1, lower=True).T
    return halve_diag(both_sides)


def shards(factor, adjoint):
    blocks_down = factor.shape[0]
    block_size = factor.shape[2]
    blocks_across = factor.shape[3]
    factor_local = factor.reshape(blocks_down, block_size, blocks_across, block_size)
    adjoint_local = adjoint.reshape(blocks_down, block_size, blocks_across, block_size)
    grid_rows = lax.axis_size("row")
    grid_cols = lax.axis_size("col")
    stride = grid_cols // grid_rows
    row_index = lax.axis_index("row")
    col_index = lax.axis_index("col")
    row_blocks = jnp.arange(blocks_down, dtype=jnp.int32) * grid_rows + row_index
    col_blocks = jnp.arange(blocks_across, dtype=jnp.int32) * grid_cols + col_index
    offsets = jnp.arange(block_size, dtype=jnp.int32)
    row_ids = row_blocks[:, None] * block_size + offsets[None, :]
    col_ids = col_blocks[:, None] * block_size + offsets[None, :]
    lower_mask = row_ids[:, :, None, None] >= col_ids[None, None, :, :]
    working = jnp.where(lower_mask, adjoint_local, 0.0)
    slot_mask = jnp.logical_and(
        jnp.arange(stride) == col_index // grid_rows, col_index % grid_rows == row_index
    ).astype(jnp.float32)

    def keep_rows(limit):
        return (row_blocks > limit).astype(jnp.float32)[:, None, None]

    for target in (1, 0):
        panel_full = broadcast(factor_local[:, :, 0, :], "col", target)
        rows_panel = panel_full * keep_rows(target)
        panel_width = rows_panel.shape[-1]
        grouped = rows_panel.reshape(blocks_across, stride, block_size, panel_width)
        picked = lax.dynamic_index_in_dim(grouped, col_index // grid_rows, axis=1, keepdims=False)
        result = broadcast(picked, "row", col_index % grid_rows)
        across = jnp.einsum(
            "aubv,bvw->auw", working, result, precision=precise, preferred_element_type=jnp.float32
        )
        mirrored = jnp.einsum(
            "aubv,auw->bvw",
            working,
            rows_panel,
            precision=precise,
            preferred_element_type=jnp.float32,
        )
        summed = lax.psum(
            mirrored * (col_blocks > target).astype(jnp.float32)[:, None, None], "row"
        )
        placed = (summed[:, None] * slot_mask[None, :, None, None]).reshape(
            blocks_down, block_size, -1
        )
        raw_sums = lax.psum(
            jnp.where(col_index == target, working[:, :, 0, :], 0.0) - across - placed, "col"
        )
        panel_sums = raw_sums * keep_rows(target)
        pivot_block = broadcast(panel_full[0][None], "row", target)[0]
        current = working
        flat_sums = panel_sums.reshape(-1, block_size)
        solved_flat = jax.scipy.linalg.solve_triangular(
            pivot_block, flat_sums.T, trans=1, lower=True
        ).T
        partial_product = jnp.dot(
            solved_flat.T,
            rows_panel.reshape(-1, block_size),
            precision=precise,
            preferred_element_type=jnp.float32,
        )
        diag_term = jnp.where(row_index == target, raw_sums[0], 0.0) - partial_product
        extra_terms = ()
        totals = lax.psum((diag_term,) + extra_terms, "row")
        diag_adjoint = cholesky_adjoint(pivot_block, jnp.tril(totals[0]))
        solved = solved_flat.reshape(blocks_down, block_size, block_size)
        column = jnp.where((row_blocks == target)[:, None, None], diag_adjoint[None], solved)
        new_column = jnp.where(col_index == target, column, current[:, :, 0, :])
        current = current.at[:, :, 0, :].set(new_column)
        working = (current, solved, diag_adjoint, totals[1:])[0]
    return working.reshape(blocks_down, 1, block_size, blocks_across, 1, block_size)


def solution(mesh):
    return jax.shard_map(
        shards,
        mesh=mesh,
        in_specs=(P(None, "row", None, None, "col", None), P(None, "row", None, None, "col", None)),
        out_specs=P(None, "row", None, None, "col", None),
        check_vma=False,
    )
```

profile of v0, /device:TPU:3, one launch (start us, length us, event | category | flops | bytes accessed | tf_op | source)
XLA Modules:
  0.0 665.0 jit_solution(11768384679800123359)
XLA Ops:
  6.5 5.0 copy.51
  11.5 2.5 select_bitcast_fusion
  14.3 7.5 %bitcast_select_fusion = f32[8,256,4,256]{3,1,0,2:T(8,128)} fusion(f32[8,1,256,4,1,256]{5,4,3,2,1,0:T(1,128)} %param.11, s32[4,256]{1,0:T(4,128)S(1)} %iota_add_fusion.1, s32[8,256]{1,0:T(8,128)S(1)} %iota_add_fusion), kind=kLoop, calls=%fused_computation.4 | loop fusion | flops 4194304 | bytes 16789504 | tf_op jit(solution)/shard_map/jit(_where)/select_n | solution.py:50
  21.8 83.4 %all-reduce.11.cloned.1.call-done = f32[8,256,256]{2,1,0:T(8,128)} async-done(((f32[8,256,256]{2,1,0:T(8,128)}), f32[8,256,256]{2,1,0:T(8,128)}) %all-reduce.11.cloned.1.call-update) | async-done | bytes 2097168 | tf_op jit(solution)/shard_map/psum | solution.py:11
  105.2 1.9 broadcast_multiply_fusion.3
  107.1 16.7 %fusion.21 = f32[4,256,256]{2,1,0:T(8,128)} fusion(f32[8,256,4,256]{3,1,0,2:T(8,128)} %bitcast_select_fusion, f32[8,256,256]{2,1,0:T(8,128)S(1)} %broadcast_multiply_fusion.3, f32[4]{0:T(128)S(1)} %compare_convert_fusion.2), kind=kOutput, calls=%fused_computation.36 | convolution fusion | flops 6442713088 | bytes 11534352 | tf_op jit(solution)/shard_map/aubv,auw->bvw/dot_general | solution.py:68
  127.0 65.6 %all-reduce.23.cloned.1.call-done = (f32[4,256,256]{2,1,0:T(8,128)}, f32[4,256,256]{2,1,0:T(8,128)}, f32[256,256]{1,0:T(8,128)}) async-done(((f32[4,256,256]{2,1,0:T(8,128)}, f32[4,256,256]{2,1,0:T(8,128)}, f32[256,256]{1,0:T(8,128)}), (f32[4,256,256]{2,1,0:T(8,128)}, f32[4,256,256]{2,1,0:T(8,128)}, f32[256,256]{1,0:T(8,128)})) %all-reduce.23.cloned.1.call-update) | async-done | bytes 2359312 | tf_op jit(solution)/shard_map/psum | solution.py:11
  192.6 10.8 %fusion.4 = f32[8,256,256]{2,1,0:T(8,128)} fusion(f32[8,256,4,256]{3,1,0,2:T(8,128)} %bitcast_select_fusion, f32[4,256,256]{2,1,0:T(8,128)} %get-tuple-element.98, f32[8]{0:T(128)S(1)} %mul.163, f32[4,256,256]{2,1,0:T(8,128)} %get-tuple-element.99, pred[]{:T(512)S(6)} %eq.65), kind=kOutput, calls=%fused_computation.19 | convolution fusion | flops 6444548096 | bytes 14680097 | tf_op jit(solution)/shard_map/aubv,bvw->auw/dot_general | solution.py:65
  203.5 7.5 %copy.67 = f32[8,256,4,256]{3,1,0,2:T(8,128)} copy(f32[8,256,4,256]{3,1,0,2:T(8,128)} %bitcast_select_fusion) | data formatting | bytes 16777216
  211.2 4.2 while.14
  215.4 19.7 %custom-call.12 = f32[2,128,128]{1,2,0:T(8,128)S(1)} custom-call(f32[2,128,128]{2,1,0:T(8,128)S(1)} %get-tuple-element.73), custom_call_target="InvertDiagBlocksLowerTriangular" | custom-call | tf_op jit(solution)/shard_map/jit(_solve_triangular)/triangular_solve | solution.py:29
  235.1 73.9 %all-reduce.19.cloned.1.call-done = (f32[8,256,256]{2,1,0:T(8,128)}, f32[8,256,256]{2,1,0:T(8,128)}) async-done(((f32[8,256,256]{2,1,0:T(8,128)}, f32[8,256,256]{2,1,0:T(8,128)}), (f32[8,256,256]{2,1,0:T(8,128)}, f32[8,256,256]{2,1,0:T(8,128)})) %all-reduce.19.cloned.1.call-update) | async-done | bytes 4194320 | tf_op jit(solution)/shard_map/psum | solution.py:81
  309.0 1.9 broadcast_multiply_fusion.2
  316.2 3.6 fusion.24
  319.8 9.7 %all-reduce.21.cloned.1.call-start = ((), (), s32[]{:S(2)}) async-start(), calls=%async_computation.5 | async-start | bytes 4718592 | tf_op jit(solution)/shard_map/psum | solution.py:11
  329.5 1.9 copy.26
  333.3 1.9 fusion.35
  336.2 41.2 %all-reduce.13.cloned.1.call-done = f32[256,256]{1,0:T(8,128)} async-done(((f32[256,256]{1,0:T(8,128)}), f32[256,256]{1,0:T(8,128)}) %all-reduce.13.cloned.1.call-update) | async-done | bytes 262160 | tf_op jit(solution)/shard_map/psum | solution.py:99
  381.0 3.4 select_dynamic-update-slice_fusion
  384.4 16.7 %fusion.18 = f32[4,256,256]{2,1,0:T(8,128)} fusion(f32[8,256,4,256]{3,1,0,2:T(8,128)} %select_dynamic-update-slice_fusion, f32[8,256,256]{2,1,0:T(8,128)S(1)} %copy-done.1, f32[4]{0:T(128)S(1)} %compare_convert_fusion), kind=kOutput, calls=%fused_computation.35 | convolution fusion | flops 6442713088 | bytes 11534352 | tf_op jit(solution)/shard_map/aubv,auw->bvw/dot_general | solution.py:68
  401.2 66.2 %all-reduce.21.cloned.1.call-done = (f32[4,256,256]{2,1,0:T(8,128)}, f32[4,256,256]{2,1,0:T(8,128)}, f32[256,256]{1,0:T(8,128)}) async-done(((f32[4,256,256]{2,1,0:T(8,128)}, f32[4,256,256]{2,1,0:T(8,128)}, f32[256,256]{1,0:T(8,128)}), (f32[4,256,256]{2,1,0:T(8,128)}, f32[4,256,256]{2,1,0:T(8,128)}, f32[256,256]{1,0:T(8,128)})) %all-reduce.21.cloned.1.call-update) | async-done | bytes 2359312 | tf_op jit(solution)/shard_map/psum | solution.py:11
  467.3 10.9 %fusion.1 = f32[8,256,256]{2,1,0:T(8,128)} fusion(f32[8,256,256]{2,1,0:T(8,128)S(1)} %bitcast.213, f32[8,256,4,256]{3,1,0,2:T(8,128)} %bitcast_select_fusion, f32[8,256,4,256]{3,1,0,2:T(8,128)} %select_dynamic-update-slice_fusion, f32[4,256,256]{2,1,0:T(8,128)} %get-tuple-element.95, f32[4,256,256]{2,1,0:T(8,128)} %get-tuple-element.96, ...), kind=kOutput, calls=%fused_computation.14 | convolution fusion | flops 6445596672 | bytes 17039402 | tf_op jit(solution)/shard_map/aubv,bvw->auw/dot_general | solution.py:65
  479.2 4.2 while.15
  483.5 19.7 %custom-call.15 = f32[2,128,128]{1,2,0:T(8,128)S(1)} custom-call(f32[2,128,128]{2,1,0:T(8,128)S(1)} %get-tuple-element.76), custom_call_target="InvertDiagBlocksLowerTriangular" | custom-call | tf_op jit(solution)/shard_map/jit(_solve_triangular)/triangular_solve | solution.py:29
  503.2 65.7 %all-reduce.15.cloned.1.call-done = f32[8,256,256]{2,1,0:T(8,128)} async-done(((f32[8,256,256]{2,1,0:T(8,128)}), f32[8,256,256]{2,1,0:T(8,128)}) %all-reduce.15.cloned.1.call-update) | async-done | bytes 2097168 | tf_op jit(solution)/shard_map/psum | solution.py:81
  571.8 2.8 convolution_subtract_fusion
  576.6 3.5 fusion.25
  580.2 2.7 fusion.8
  582.9 3.0 copy.33
  585.9 53.2 %all-reduce.17.cloned.1.call-done = f32[256,256]{1,0:T(8,128)} async-done(((f32[256,256]{1,0:T(8,128)}), f32[256,256]{1,0:T(8,128)}) %all-reduce.17.cloned.1.call-update) | async-done | bytes 262160 | tf_op jit(solution)/shard_map/psum | solution.py:99
  642.7 4.1 bitcast_dynamic-update-slice_fusion.2
  646.8 11.0 %copy.36 = f32[8,1,256,4,1,256]{5,4,3,2,1,0:T(1,128)} copy(f32[8,1,256,4,1,256]{5,2,0,3,4,1:T(8,128)} %bitcast_dynamic-update-slice_fusion.2) | data formatting | bytes 16777216 | tf_op jit(solution)/shard_map/scatter | solution.py:104
  (93 shorter events, 33.1 us)
Async XLA Ops:
  6.5 98.7 %all-reduce.11.cloned.1.call-start = ((), (), s32[]{:S(2)}) async-start(), calls=%async_computation | async-start | bytes 4194304 | tf_op jit(solution)/shard_map/psum | solution.py:11
  14.1 178.6 %all-reduce.23.cloned.1.call-start = ((), (), s32[]{:S(2)}) async-start(), calls=%async_computation.6 | async-start | bytes 4718592 | tf_op jit(solution)/shard_map/psum | solution.py:11
  126.6 182.4 %all-reduce.19.cloned.1.call-start = ((), (), s32[]{:S(2)}) async-start(), calls=%async_computation.4 | async-start | bytes 8388608 | tf_op jit(solution)/shard_map/psum | solution.py:81
  203.4 174.0 %all-reduce.13.cloned.1.call-start = ((), (), s32[]{:S(2)}) async-start(), calls=%async_computation.1 | async-start | bytes 524288 | tf_op jit(solution)/shard_map/psum | solution.py:99
  203.5 7.6 %copy-start.6 = (f32[256,256]{1,0:T(8,128)S(1)}, f32[256,256]{1,0:T(8,128)}, u32[]{:S(2)}) copy-start(f32[256,256]{1,0:T(8,128)} %get-tuple-element.100) | copy-start | bytes 786436
  319.8 147.5 %all-reduce.21.cloned.1.call-start = ((), (), s32[]{:S(2)}) async-start(), calls=%async_computation.5 | async-start | bytes 4718592 | tf_op jit(solution)/shard_map/psum | solution.py:11
  333.3 1.9 copy-start
  381.0 3.4 copy-start.1
  401.1 167.7 %all-reduce.15.cloned.1.call-start = ((), (), s32[]{:S(2)}) async-start(), calls=%async_computation.2 | async-start | bytes 4194304 | tf_op jit(solution)/shard_map/psum | solution.py:81
  478.2 0.9 copy-start.7
  478.3 160.9 %all-reduce.17.cloned.1.call-start = ((), (), s32[]{:S(2)}) async-start(), calls=%async_computation.3 | async-start | bytes 524288 | tf_op jit(solution)/shard_map/psum | solution.py:99
  483.5 87.2 %copy-start.4 = (f32[256,256]{1,0:T(8,128)}, f32[256,256]{1,0:T(8,128)S(1)}, u32[]{:S(2)}) copy-start(f32[256,256]{1,0:T(8,128)S(1)} %get-tuple-element.234) | copy-start | bytes 786436
  571.7 4.9 copy-start.2
  575.6 1.0 copy-start.3
  582.9 56.2 %copy-start.8 = (f32[256,256]{1,0:T(8,128)S(1)}, f32[256,256]{1,0:T(8,128)}, u32[]{:S(2)}) copy-start(f32[256,256]{1,0:T(8,128)} %get-tuple-element.97) | copy-start | bytes 786436
  582.9 58.0 %copy-start.5 = (f32[256,256]{1,0:T(8,128)S(1)}, f32[256,256]{1,0:T(8,128)}, u32[]{:S(2)}) copy-start(f32[256,256]{1,0:T(8,128)} %copy-done.4) | copy-start | bytes 786436
Sparse Core Ops, SparseCore 0:
  14.2 91.0 all-reduce.10
  126.7 65.8 all-reduce.22
  203.6 105.3 all-reduce.18
  319.9 57.4 all-reduce.12
  401.2 66.0 all-reduce.20
  478.4 90.3 all-reduce.14
  580.3 58.7 all-reduce.16
where the time goes:
time: 676 us; the launch traced here: 665 us
  waiting for transfers between devices  449 us (66%)
  matrix products  77.5 us (11%)
  other arithmetic  74.6 us (11%)
  local copies, waits for them, and re-layouts  38.8 us (6%)
  between operations  14.4 us (2%)
  starting transfers between devices  10.3 us (2%)
    psum x3, waiting for transfers between devices, broadcast(): return lax.psum(block, axis)  215 us
    psum x2, waiting for transfers between devices, shards(): lax.psum(jnp.where(col_index == target, working[:, :, 0, :], 0.0) - acros...  140 us
    psum x2, waiting for transfers between devices, shards(): totals = lax.psum((diag_term,) + extra_terms, 'row')  94.4 us
    another operation x5, other arithmetic, cholesky_adjoint(): jax.scipy.linalg.solve_triangular(pivot_block, left_side.T, trans=1, lowe...  39.4 us
    dot_general x2, matrix products, shards(): jnp.einsum('aubv,auw->bvw', working, rows_panel, precision=precise, prefe...  33.3 us
    dot_general x2, matrix products, shards(): jnp.einsum('aubv,bvw->auw', working, result, precision=precise, preferred...  21.7 us
    unnamed x20, local copies, waits for them, and re-layouts  14.2 us
  transfers between devices with their start and end apart: 7, of which 7 were waited for; matrix products, arithmetic and copies ran while one was open for 11% of the time, Pallas kernels for 0%

commit v1 on v0

v1 whole, which is shorter than its diff:
```python
import jax
import jax.numpy as jnp
from jax import lax
from jax.experimental import pallas as pl
from jax.experimental.pallas import tpu as pltpu
from jax.sharding import PartitionSpec as P

F32, BF16 = jnp.float32, jnp.bfloat16
MESH = pl.DeviceIdType.MESH
precise = lax.Precision.HIGHEST


def up(v):
    return lax.rem(v + 1, 4)


def down(v):
    return lax.rem(v + 3, 4)


def across_from(v):
    return lax.rem(v + 2, 4)


def split(value):
    high = value.astype(BF16)
    return high, (value - high.astype(F32)).astype(BF16)


def dot(left, right):
    return jnp.dot(left, right, preferred_element_type=F32)


def dot3(left, right):
    (left_high, left_low), (right_high, right_low) = left, right
    return dot(left_high, right_high) + (dot(left_high, right_low) + dot(left_low, right_high))


def exact(left, right):
    return jnp.dot(left, right, precision=precise, preferred_element_type=F32)


def iotas(shape):
    return (
        lax.broadcasted_iota(jnp.int32, shape, 0),
        lax.broadcasted_iota(jnp.int32, shape, 1),
    )


def lower(matrix):
    row, col = iotas(matrix.shape)
    return jnp.where(row >= col, matrix, 0.0)


def halve_diag(matrix):
    row, col = iotas(matrix.shape)
    return jnp.where(row > col, matrix, jnp.where(row == col, 0.5 * matrix, 0.0))


def inverses(blocks):
    row, col = iotas(blocks[0].shape)
    found = [jnp.where(row == col, 1.0 / jnp.where(row == col, q, 1.0), 0.0) for q in blocks]
    size = 1
    while size < blocks[0].shape[0]:
        here = jnp.logical_and(row // (2 * size) == col // (2 * size), row // size > col // size)
        left = [exact(x, jnp.where(here, q, 0.0)) for x, q in zip(found, blocks)]
        found = [x - exact(y, x) for x, y in zip(found, left)]
        size *= 2
    return found


def diag_step(pivot, inverse, target):
    inner = halve_diag(exact(pivot.T, target))
    return halve_diag(exact(exact(inverse.T, inner), inverse))


def sweep_kernel(
    panel,
    adj,
    out,
    s_ref,
    crow,
    ccol,
    ct,
    sw,
    cc,
    oacc,
    macc,
    mate_in,
    yopp,
    ynbr,
    moved,
    opp1,
    nbr1,
    opp2,
    nbr2,
    agath,
    apiece,
    qbuf,
    qinv,
    tbuf,
    trecv,
    tslice,
    tall1,
    tall0,
    rblk,
    rsend,
    done,
    a01,
    local_sem,
    scat_s,
    scat_r,
    ag1,
    ag2,
    chain_s,
    chain_r,
    q_s,
    q_r,
    ring,
    mate_sem,
    moved_sem,
    ga_s,
    ga_r,
    t_s,
    t_r,
    root_s,
    root_r,
    blk_sem,
):
    r, c = lax.axis_index("row"), lax.axis_index("col")
    y, core = lax.div(r, 2), lax.rem(r, 2)
    z, x = lax.div(c, 4), lax.rem(c, 4)
    place = ((x, z), (z, x))
    home = lax.rem(c, 8)
    home_y, home_core = lax.div(home, 2), lax.rem(home, 2)
    group = lax.div(c, 8)
    mate = (y * 2 + 1 - core, c)
    target = (home, 4 * y + 2 * group + core)
    giver = (2 * z + lax.rem(x, 2), r + 8 * lax.div(x, 2))
    pending = []

    def piece(p, first, second):
        return second * 4 + first if p == 0 else first * 4 + second

    def member(p, first, second):
        return (r, piece(p, first, second))

    def send(src, dst, ss, rs, device):
        copy = pltpu.make_async_remote_copy(
            src_ref=src, dst_ref=dst, send_sem=ss, recv_sem=rs, device_id=device, device_id_type=MESH
        )
        copy.start()
        return copy

    def post(*args):
        pending.append(send(*args))

    def arrived(dst, rs):
        pltpu.make_async_remote_copy(
            src_ref=dst, dst_ref=dst, send_sem=rs, recv_sem=rs, device_id=mate, device_id_type=MESH
        ).wait_recv()

    def left(src, ss):
        pltpu.make_async_remote_copy(
            src_ref=src, dst_ref=src, send_sem=ss, recv_sem=ss, device_id=mate, device_id_type=MESH
        ).wait_send()

    load = pltpu.make_async_copy(adj, s_ref, local_sem.at[0])
    load.start()

    barrier = pltpu.get_barrier_semaphore()

    def greet(device):
        pl.semaphore_signal(barrier, inc=1, device_id=device, device_id_type=MESH)

    for step in range(1, 16):
        greet((r, lax.rem(c + step, 16)))
    for step in range(1, 8):
        greet((lax.rem(r + step, 8), c))
    away = jnp.logical_or(target[0] != r, target[1] != c)
    from_away = jnp.logical_or(giver[0] != r, giver[1] != c)
    is_root = jnp.logical_and(r == 0, c == 0)
    owes_root = jnp.logical_and(r > 0, c == 1)

    @pl.when(from_away)
    def _():
        greet(giver)

    @pl.when(is_root)
    def _():
        for step in range(1, 8):
            greet((step, 1))

    pl.semaphore_wait(barrier, 22 + jnp.where(away, 1, 0) + jnp.where(owes_root, 1, 0))

    order = (10, 11, 14, 15, 6, 7, 8, 9, 12, 13, 2, 3, 5, 4, 1, 0)
    for p in range(2):

        @pl.when(c == p)
        def _():
            for k in order:
                if k != p:
                    send(panel.at[k], crow.at[p, k], scat_s.at[k], scat_r.at[p], (r, k))
            own = pltpu.make_async_copy(panel.at[p], crow.at[p, p], local_sem.at[1])
            own.start()
            own.wait()

    def halves(ref, half):
        return ref.at[pl.ds(64 * half, 64)]

    def gather_second(p, q, first):
        f, s = place[p]
        held = crow.at[p, piece(p, first, s)]
        post(held, held, ag2.at[0, p, q, 0], ag2.at[1, p, q, 0], member(p, f, up(s)))
        post(held, held, ag2.at[0, p, q, 1], ag2.at[1, p, q, 1], member(p, f, down(s)))

    for p in range(2):
        f, s = place[p]
        held = crow.at[p, piece(p, f, s)]

        @pl.when(c != p)
        def _():
            arrived(crow.at[p, c], scat_r.at[p])

        post(held, held, ag1.at[0, p, 0], ag1.at[1, p, 0], member(p, up(f), s))
        post(held, held, ag1.at[0, p, 1], ag1.at[1, p, 1], member(p, down(f), s))
        gather_second(p, 0, f)
    for p in range(2):
        f, s = place[p]
        held = crow.at[p, piece(p, down(f), s)]
        arrived(held, ag1.at[1, p, 0])
        part = halves(held, 0)
        post(part, part, ag1.at[0, p, 2], ag1.at[1, p, 2], member(p, up(f), s))
        gather_second(p, 1, down(f))
        held = crow.at[p, piece(p, up(f), s)]
        arrived(held, ag1.at[1, p, 1])
        part = halves(held, 1)
        post(part, part, ag1.at[0, p, 3], ag1.at[1, p, 3], member(p, down(f), s))
        gather_second(p, 2, up(f))
    for p in range(2):
        f, s = place[p]
        held = crow.at[p, piece(p, across_from(f), s)]
        arrived(halves(held, 0), ag1.at[1, p, 2])
        arrived(halves(held, 1), ag1.at[1, p, 3])
        gather_second(p, 3, across_from(f))
    for q in range(4):
        for p in range(2):
            f, s = place[p]
            first = (f, down(f), up(f), across_from(f))[q]
            held = crow.at[p, piece(p, first, down(s))]
            arrived(held, ag2.at[1, p, q, 0])
            part = halves(held, 0)
            post(part, part, ag2.at[0, p, q, 2], ag2.at[1, p, q, 2], member(p, f, up(s)))
            held = crow.at[p, piece(p, first, up(s))]
            arrived(held, ag2.at[1, p, q, 1])
            part = halves(held, 1)
            post(part, part, ag2.at[0, p, q, 3], ag2.at[1, p, q, 3], member(p, f, down(s)))
    for q in range(4):
        for p in range(2):
            f, s = place[p]
            first = (f, down(f), up(f), across_from(f))[q]
            held = crow.at[p, piece(p, first, across_from(s))]
            arrived(halves(held, 0), ag2.at[1, p, q, 2])
            arrived(halves(held, 1), ag2.at[1, p, q, 3])

    load.wait()

    in_line = core == home_core
    is_home = jnp.logical_and(in_line, y == home_y)
    relays = jnp.logical_and(in_line, y != home_y)
    next_y = (up(y), down(y))
    gap = (lax.rem(y - home_y + 4, 4), lax.rem(home_y - y + 4, 4))

    def home_pieces(p, b):
        return crow.at[p, pl.ds(4 * b + 2 * group, 2)]

    chunks = [(p, b) for b in range(4) for p in range(2)]

    @pl.when(is_home)
    def _():
        for p, b in chunks:
            src = home_pieces(p, b)
            send(src, ccol.at[p, b], chain_s.at[p, b, 0], chain_r.at[p, b], (next_y[p] * 2 + core, c))
            send(src, ccol.at[p, b], chain_s.at[p, b, 1], chain_r.at[p, b], mate)
            pltpu.make_async_copy(src, ccol.at[p, b], local_sem.at[2 + p * 4 + b]).start()

    def relay(p, b):
        @pl.when(relays)
        def _():
            held = ccol.at[p, b]
            arrived(held, chain_r.at[p, b])

            @pl.when(gap[p] < 3)
            def _():
                send(held, held, chain_s.at[p, b, 0], chain_r.at[p, b], (next_y[p] * 2 + core, c))

            send(held, held, chain_s.at[p, b, 1], chain_r.at[p, b], mate)

    pivots = ((0, 0, 0), (1, 0, 1), (2, 1, 1))

    for slot, p, holder in pivots:

        @pl.when(r == holder)
        def _():
            src = crow.at[p, pl.ds(0, 2)]
            send(src, qbuf.at[slot], q_s.at[slot, 0], q_r.at[slot], (2 + holder, c))
            send(src, qbuf.at[slot], q_s.at[slot, 1], q_r.at[slot], (6 + holder, c))
            send(src, qbuf.at[slot], q_s.at[slot, 2], q_r.at[slot], (4 + holder, c))
            send(src, qbuf.at[slot], q_s.at[slot, 3], q_r.at[slot], mate)
            own = pltpu.make_async_copy(src, qbuf.at[slot], local_sem.at[1])
            own.start()
            own.wait()

    def adjoint_block(a, b):
        return jnp.concatenate(
            [s_ref[pl.ds(a * 2048 + 2 * b + h, 256, stride=8), :] for h in range(2)], axis=1
        )

    at_11 = jnp.logical_and(r == 1, c == 1)
    at_10 = jnp.logical_and(r == 1, c == 0)

    @pl.when(at_11)
    def _():
        rsend[...] = adjoint_block(0, 0)
        send(rsend, rblk.at[0], blk_sem.at[0], blk_sem.at[2], (0, 0))

    @pl.when(at_10)
    def _():
        rsend[...] = adjoint_block(0, 0)
        send(rsend, rblk.at[1], blk_sem.at[1], blk_sem.at[3], (0, 0))

    row_iota, col_iota = iotas((256, 256))

    def active(a, b):
        i, j = 8 * a + r, 16 * b + c
        return jnp.logical_and(j >= 2, j <= i)

    macc[...] = jnp.zeros_like(macc)

    def mirrored(a):
        for p in range(2):
            for half in range(2):
                high, low = split(crow[p, 2 * a + half])
                lanes = pl.ds(128 * half, 128)
                ct[0, pl.ds(256 * p, 256), lanes] = high.T
                ct[1, pl.ds(256 * p, 256), lanes] = low.T

        def per_block(b, carry):
            @pl.when(active(a, b))
            def _():
                shift = 256 * (8 * a + r - 16 * b - c)
                block = jnp.where(row_iota + shift >= col_iota, adjoint_block(a, b), 0.0)
                high, low = split(block)
                sw[0, a, b] = high
                sw[1, a, b] = low
                total = dot3((ct[0], ct[1]), (high, low))
                macc[b, 0] += total[:, :128]
                macc[b, 1] += total[:, 128:]

            return carry

        lax.fori_loop(0, 4, per_block, 0)

    for step, (p, b) in enumerate(chunks):
        mirrored(step)
        relay(p, b)

    for b in range(4):
        post(
            macc.at[b, 1 - core], mate_in.at[b], mate_sem.at[0, b], mate_sem.at[1, b], mate
        )

    @pl.when(is_home)
    def _():
        for p, b in chunks:
            pltpu.make_async_copy(home_pieces(p, b), ccol.at[p, b], local_sem.at[2 + p * 4 + b]).wait()

    @pl.when(jnp.logical_not(in_line))
    def _():
        for p, b in chunks:
            arrived(ccol.at[p, b], chain_r.at[p, b])

    def ready_columns(b, carry):
        for p in range(2):
            for half in range(2):
                high, low = split(ccol[p, b, half])
                rows, lanes = pl.ds(128 * half, 128), pl.ds(256 * p, 256)
                cc[0, b, rows, lanes] = high
                cc[1, b, rows, lanes] = low
        return carry

    lax.fori_loop(0, 4, ready_columns, 0)

    oacc[...] = jnp.zeros_like(oacc)

    def direct(a, carry):
        for p in range(2):

            @pl.when(c == p)
            def _():
                block = adjoint_block(a, 0)
                oacc[p, 2 * a] = -block[:128]
                oacc[p, 2 * a + 1] = -block[128:]

        def per_block(b, inner):
            @pl.when(active(a, b))
            def _():
                total = dot3((sw[0, a, b], sw[1, a, b]), (cc[0, b], cc[1, b]))
                for p in range(2):
                    for half in range(2):
                        oacc[p, 2 * a + half] += total[128 * half : 128 * half + 128, 256 * p : 256 * p + 256]

            return inner

        lax.fori_loop(0, 4, per_block, 0)
        return carry

    lax.fori_loop(0, 8, direct, 0)

    def ring_open(slot, held, pos, device, rows, opp, nbr):
        def part(ref, half):
            return ref.at[pl.ds(rows * half, rows)]

        def go(src, dst, n, where):
            post(src, dst, ring.at[0, slot, n], ring.at[1, slot, n], device(where))

        far = held(across_from(pos))
        go(part(far, 0), opp.at[0], 0, down(pos))
        go(part(far, 1), opp.at[1], 1, up(pos))
        go(part(held(down(pos)), 1), part(nbr.at[0], 1), 2, down(pos))
        go(part(held(up(pos)), 0), part(nbr.at[1], 0), 3, up(pos))

    def ring_pass(slot, held, pos, device, rows, opp, nbr):
        def part(ref, half):
            return ref.at[pl.ds(rows * half, rows)]

        def go(src, dst, n, where):
            post(src, dst, ring.at[0, slot, n], ring.at[1, slot, n], device(where))

        arrived(opp.at[0], ring.at[1, slot, 0])
        mine = part(held(down(pos)), 0)
        mine[...] = mine[...] + opp[0]
        go(mine, part(nbr.at[0], 0), 4, down(pos))
        arrived(opp.at[1], ring.at[1, slot, 1])
        mine = part(held(up(pos)), 1)
        mine[...] = mine[...] + opp[1]
        go(mine, part(nbr.at[1], 1), 5, up(pos))

    def ring_close(slot, held, pos, device, rows, opp, nbr):
        def part(ref, half):
            return ref.at[pl.ds(rows * half, rows)]

        arrived(part(nbr.at[0], 1), ring.at[1, slot, 2])
        arrived(part(nbr.at[0], 0), ring.at[1, slot, 4])
        arrived(part(nbr.at[1], 0), ring.at[1, slot, 3])
        arrived(part(nbr.at[1], 1), ring.at[1, slot, 5])
        mine = held(pos)
        mine[...] = mine[...] + (nbr[0] + nbr[1])

    def first_ring(p, j):
        f, s = place[p]
        return (
            4 * p + j,
            lambda t: oacc.at[p, piece(p, j, t)],
            s,
            lambda t: member(p, f, t),
            64,
            opp1.at[p, j],
            nbr1.at[p, j],
        )

    def second_ring(p):
        f, s = place[p]
        return (
            8 + p,
            lambda t: oacc.at[p, piece(p, t, s)],
            f,
            lambda t: member(p, t, s),
            64,
            opp2.at[p],
            nbr2.at[p],
        )

    column_ring = (
        10,
        lambda t: macc.at[t, core],
        y,
        lambda t: (t * 2 + core, c),
        256,
        yopp,
        ynbr,
    )
    rings = [first_ring(p, j) for j in range(4) for p in range(2)]
    for spec in rings:
        ring_open(*spec)

    for b in range(4):
        arrived(mate_in.at[b], mate_sem.at[1, b])
    for b in range(4):
        mine = macc.at[b, core]
        mine[...] = mine[...] + mate_in[b]
    ring_open(*column_ring)

    for spec in rings:
        ring_pass(*spec)
    ring_pass(*column_ring)

    for slot, p, holder in pivots:

        @pl.when(r != holder)
        def _():
            arrived(qbuf.at[slot], q_r.at[slot])

            @pl.when(core == holder)
            def _():
                send(qbuf.at[slot], qbuf.at[slot], q_s.at[slot, 3], q_r.at[slot], mate)

    def pivot(slot):
        return jnp.concatenate([qbuf[slot, 0], qbuf[slot, 1]], axis=0)

    inverse_0, inverse_1 = inverses([pivot(0), pivot(2)])
    qinv[0] = inverse_0
    qinv[1] = inverse_1

    for spec in rings:
        ring_close(*spec)
    for p in range(2):
        ring_open(*second_ring(p))
    ring_close(*column_ring)

    @pl.when(away)
    def _():
        send(macc.at[y, core], moved, moved_sem.at[0], moved_sem.at[1], target)

    @pl.when(jnp.logical_not(away))
    def _():
        moved[...] = macc[y, core]

    for p in range(2):
        ring_pass(*second_ring(p))
    for p in range(2):
        ring_close(*second_ring(p))

    @pl.when(from_away)
    def _():
        arrived(moved, moved_sem.at[1])

    keep = jnp.where(jnp.logical_and(c < 2, r < 2), 0.0, -1.0)
    extra = moved[...].T
    sums_1 = (oacc[1, c] + extra[:, 256:]) * keep
    sums_0 = (oacc[0, c] + extra[:, :256]) * keep
    solved_1 = exact(sums_1, qinv[1])
    apiece[1] = solved_1

    def hand_in(p):
        @pl.when(c != p)
        def _():
            send(apiece.at[p], agath.at[c], ga_s.at[p], ga_r.at[c], (r, p))

    hand_in(1)
    solved_0 = exact(sums_0 - exact(solved_1, pivot(1)), qinv[0])
    apiece[0] = solved_0
    hand_in(0)

    @pl.when(c < 2)
    def _():
        for p in range(2):

            @pl.when(c == p)
            def _():
                agath[p] = apiece[p]

                for k in range(16):
                    if k != p:
                        arrived(agath.at[k], ga_r.at[k])

        def gathered(k, total):
            high, low = split(agath[k])
            sides = (high.T, low.T)
            first = dot3(sides, split(crow[c, k]))
            second = dot3(sides, split(crow[0, k]))
            return total[0] + first, total[1] + second

        zero = jnp.zeros((256, 256), F32)
        total = lax.fori_loop(0, 16, gathered, (zero, zero))
        for t in range(8):
            for n in range(2):
                tbuf[t, n] = total[n][32 * t : 32 * t + 32]
        for step in range(1, 8):
            to = lax.rem(r + step, 8)
            send(tbuf.at[to], trecv.at[step], t_s.at[step], t_r.at[step], (to, c))
        result = tbuf[r]
        for step in range(1, 8):
            arrived(trecv.at[step], t_r.at[step])
            result = result + trecv[step]
        tslice[...] = result

        @pl.when(c == 1)
        def _():
            send(tslice, tall1.at[r], root_s.at[0], root_r.at[0, r], (0, 0))

            @pl.when(r != 1)
            def _():
                send(tslice, tall1.at[r], root_s.at[1], root_r.at[0, r], (1, 1))

        @pl.when(jnp.logical_and(c == 0, r != 0))
        def _():
            send(tslice.at[0], tall0.at[r], root_s.at[0], root_r.at[1, r], (0, 0))

    def flat(parts):
        return jnp.concatenate(parts, axis=0)

    @pl.when(at_11)
    def _():
        tall1[1] = tslice[...]
        for t in range(8):
            if t != 1:
                arrived(tall1.at[t], root_r.at[0, t])
        sums = flat([tall1[t, 0] for t in range(8)])
        done[...] = diag_step(pivot(2), qinv[1], lower(adjoint_block(0, 0) - sums))

    @pl.when(is_root)
    def _():
        tall0[0] = tslice[0]
        for t in range(8):
            arrived(tall1.at[t], root_r.at[0, t])
        arrived(rblk.at[0], blk_sem.at[2])
        arrived(rblk.at[1], blk_sem.at[3])
        sums = flat([tall1[t, 0] for t in range(8)])
        diag_1 = diag_step(pivot(2), qinv[1], lower(rblk[0] - sums))
        cross = flat([tall1[t, 1] for t in range(8)])
        link = pivot(1)
        rows_1 = exact(rblk[1] - cross - exact(diag_1 + diag_1.T, link), qinv[0])
        rsend[...] = rows_1
        send(rsend, a01, blk_sem.at[4], blk_sem.at[5], (1, 0))
        for t in range(1, 8):
            arrived(tall0.at[t], root_r.at[1, t])
        sums = flat([tall0[t] for t in range(8)]) + exact(rows_1.T, link)
        done[...] = diag_step(pivot(0), qinv[0], lower(adjoint_block(0, 0) - sums))
        left(rsend, blk_sem.at[4])

    @pl.when(at_10)
    def _():
        arrived(a01, blk_sem.at[5])
        done[...] = a01[...]

    @pl.when(c < 2)
    def _():
        def write(k, carry):
            value = agath[k]
            for h in range(2):
                out[pl.ds(256 * k + h, 128, stride=2), :] = value[:, 128 * h : 128 * h + 128]
            return carry

        lax.fori_loop(0, 16, write, 0)

        @pl.when(jnp.logical_and(r < 2, jnp.logical_or(r == 1, c == 0)))
        def _():
            value = done[...]
            for h in range(2):
                out[pl.ds(h, 256, stride=2), :] = value[:, 128 * h : 128 * h + 128]

    @pl.when(c >= 2)
    def _():
        out[...] = jnp.zeros_like(out)

    for copy in pending:
        copy.wait_send()
    for p in range(2):

        @pl.when(c == p)
        def _():
            for k in range(16):
                if k != p:
                    left(panel.at[k], scat_s.at[k])

        @pl.when(c != p)
        def _():
            left(apiece.at[p], ga_s.at[p])

    for p, b in chunks:

        @pl.when(in_line)
        def _():
            left(ccol.at[p, b], chain_s.at[p, b, 1])

            @pl.when(gap[p] < 3)
            def _():
                left(ccol.at[p, b], chain_s.at[p, b, 0])

    for slot, p, holder in pivots:

        @pl.when(core == holder)
        def _():
            left(qbuf.at[slot], q_s.at[slot, 3])

        @pl.when(r == holder)
        def _():
            for n in range(3):
                left(qbuf.at[slot], q_s.at[slot, n])

    @pl.when(at_11)
    def _():
        left(rsend, blk_sem.at[0])

    @pl.when(at_10)
    def _():
        left(rsend, blk_sem.at[1])

    @pl.when(away)
    def _():
        left(moved, moved_sem.at[0])

    @pl.when(c < 2)
    def _():
        for step in range(1, 8):
            left(trecv.at[step], t_s.at[step])

        @pl.when(c == 1)
        def _():
            left(tslice, root_s.at[0])

            @pl.when(r != 1)
            def _():
                left(tslice, root_s.at[1])

        @pl.when(jnp.logical_and(c == 0, r != 0))
        def _():
            left(tslice.at[0], root_s.at[0])


def sweep(panel, adj):
    vmem = pltpu.VMEM
    dma = pltpu.SemaphoreType.DMA
    return pl.pallas_call(
        sweep_kernel,
        out_shape=jax.ShapeDtypeStruct((4096, 128), F32),
        in_specs=[pl.BlockSpec(memory_space=pl.ANY)] * 2,
        out_specs=pl.BlockSpec(memory_space=pltpu.VMEM),
        scratch_shapes=[
            vmem((16384, 128), F32),
            vmem((2, 16, 128, 256), F32),
            vmem((2, 4, 2, 128, 256), F32),
            vmem((2, 512, 256), BF16),
            vmem((2, 8, 4, 256, 256), BF16),
            vmem((2, 4, 256, 512), BF16),
            vmem((2, 16, 128, 256), F32),
            vmem((4, 2, 512, 128), F32),
            vmem((4, 512, 128), F32),
            vmem((2, 256, 128), F32),
            vmem((2, 512, 128), F32),
            vmem((512, 128), F32),
            vmem((2, 4, 2, 64, 256), F32),
            vmem((2, 4, 2, 128, 256), F32),
            vmem((2, 2, 64, 256), F32),
            vmem((2, 2, 128, 256), F32),
            vmem((16, 128, 256), F32),
            vmem((2, 128, 256), F32),
            vmem((3, 2, 128, 256), F32),
            vmem((2, 256, 256), F32),
            vmem((8, 2, 32, 256), F32),
            vmem((8, 2, 32, 256), F32),
            vmem((2, 32, 256), F32),
            vmem((8, 2, 32, 256), F32),
            vmem((8, 32, 256), F32),
            vmem((2, 256, 256), F32),
            vmem((256, 256), F32),
            vmem((256, 256), F32),
            vmem((256, 256), F32),
            dma((10,)),
            dma((16,)),
            dma((2,)),
            dma((2, 2, 4)),
            dma((2, 2, 4, 4)),
            dma((2, 4, 2)),
            dma((2, 4)),
            dma((3, 4)),
            dma((3,)),
            dma((2, 11, 6)),
            dma((2, 4)),
            dma((2,)),
            dma((2,)),
            dma((16,)),
            dma((8,)),
            dma((8,)),
            dma((2,)),
            dma((2, 8)),
            dma((6,)),
        ],
        compiler_params=pltpu.CompilerParams(
            collective_id=0, has_side_effects=True, vmem_limit_bytes=60 * 2**20
        ),
        name="sweep",
    )(panel, adj)


def merge_kernel(adj, panel, out):
    r, c = lax.axis_index("row"), lax.axis_index("col")
    a = pl.program_id(0)
    shape = (256, 8, 128)
    slot = lax.broadcasted_iota(jnp.int32, (1, 8, 128), 1)
    lane = lax.broadcasted_iota(jnp.int32, (1, 8, 128), 2)
    col = (16 * (slot // 2) + c) * 256 + lax.rem(slot, 2) * 128 + lane
    row = (8 * a + r) * 256 + lax.broadcasted_iota(jnp.int32, shape, 0)
    value = jnp.where(row >= col, adj[...].reshape(shape), 0.0)
    out[...] = value.reshape(2048, 128)

    @pl.when(c < 2)
    def _():
        for h in range(2):
            out[pl.ds(h, 256, stride=8), :] = panel[pl.ds(h, 256, stride=2), :]


def merge(adj, panel):
    return pl.pallas_call(
        merge_kernel,
        grid=(8,),
        out_shape=jax.ShapeDtypeStruct((16384, 128), F32),
        in_specs=[
            pl.BlockSpec((2048, 128), lambda a: (a, 0)),
            pl.BlockSpec((512, 128), lambda a: (a, 0)),
        ],
        out_specs=pl.BlockSpec((2048, 128), lambda a: (a, 0)),
        compiler_params=pltpu.CompilerParams(vmem_limit_bytes=32 * 2**20),
        name="merge",
    )(adj, panel)


def shards(factor, adjoint):
    panel = factor[:, 0, :, 0, 0, :].reshape(16, 128, 256)
    adj = adjoint.reshape(16384, 128)
    solved = sweep(panel, adj)
    return merge(adj, solved).reshape(adjoint.shape)


def solution(mesh):
    spec = P(None, "row", None, None, "col", None)
    return jax.shard_map(
        shards,
        mesh=mesh,
        in_specs=(spec, spec),
        out_specs=spec,
        check_vma=False,
    )
```

time: 676 us -> 269 us (0.40)
  waiting for transfers between devices: 449 us -> 0 us
  Pallas kernels: 0 us -> 255 us
  matrix products: 77.5 us -> 0 us
  other arithmetic: 74.6 us -> 0 us
  local copies, waits for them, and re-layouts: 38.8 us -> 9.55 us
  between operations: 14.4 us -> 0.02 us
  starting transfers between devices: 10.3 us -> 0 us
    psum x7 -> x0, waiting for transfers between devices: 449 us -> none  [the longest x3 215 us: broadcast(): return lax.psum(block, axis)]
    pallas_call x0 -> x2, Pallas kernels: none -> 255 us  [the longest x1 250 us: sweep(): pl.pallas_call(sweep_kernel, out_shape=jax.ShapeDtypeStruct((4096, 128),...]
    dot_general x8 -> x0, matrix products: 65.2 us -> none  [the longest x2 33.3 us: shards(): jnp.einsum('aubv,auw->bvw', working, rows_panel, precision=precise, prefe...]
    another operation x5 -> x0, other arithmetic: 39.4 us -> none  [cholesky_adjoint(): jax.scipy.linalg.solve_triangular(pivot_block, left_side.T, trans=1, lowe...]
    another operation x18 -> x0, matrix products: 12.3 us -> none  [the longest x6 8.71 us: shards(): jax.scipy.linalg.solve_triangular(pivot_block, flat_sums.T, trans=1, lowe...]
    select_n x4 -> x0, other arithmetic: 12.1 us -> none  [the longest x1 7.5 us: shards(): working = jnp.where(lower_mask, adjoint_local, 0.0)]
    scatter x1 -> x0, local copies, waits for them, and re-layouts: 11 us -> none  [shards(): current = current.at[:, :, 0, :].set(new_column)]
    psum x7 -> x0, starting transfers between devices: 10.3 us -> none  [the longest x3 9.71 us: broadcast(): return lax.psum(block, axis)]
  transfers between devices with their start and end apart: 7 -> 0, of which waited for: 7 -> 0; matrix products, arithmetic and copies ran while one was open for 11% -> 0% of each run, Pallas kernels for 0% -> 0%
where the time goes in v1:
time: 269 us; the launch traced here: 265 us
  Pallas kernels  255 us (95%)
  local copies, waits for them, and re-layouts  9.55 us (4%)
    pallas_call x1, Pallas kernels, sweep(): pl.pallas_call(sweep_kernel, out_shape=jax.ShapeDtypeStruct((4096, 128),...  250 us
    unnamed x5, local copies, waits for them, and re-layouts  6.52 us

profile of v1, /device:TPU:3, one launch (start us, length us, event | category | flops | bytes accessed | tf_op | source)
XLA Modules:
  0.0 264.6 jit_solution(9614587418994953001)
XLA Ops:
  0.0 3.0 %slice.3 = f32[8,1,256,1,1,256]{5,4,3,2,1,0:T(1,128)S(1)} slice(f32[8,1,256,4,1,256]{5,4,3,2,1,0:T(1,128)} %param.2), slice={[0:8], [0:1], [0:256], [0:1], [0:1], [0:256]} | slice | bytes 4194304 | tf_op jit(solution)/shard_map/slice | solution.py:830
  3.0 1.5 copy.4
  4.6 250.0 %sweep.1.panel = f32[4096,128]{1,0:T(8,128)} custom-call(f32[16,128,256]{2,1,0:T(8,128)} %bitcast.5, f32[16384,128]{1,0:T(8,128)} %bitcast.3), custom_call_target="tpu_custom_call" | custom-call | tf_op jit(solution)/shard_map/sweep/pallas_call | solution.py:735
  254.6 0.0 copy-start
  254.7 3.4 %copy-done = f32[8,1,256,4,1,256]{5,4,3,2,1,0:T(1,128)S(1)} copy-done((f32[8,1,256,4,1,256]{5,4,3,2,1,0:T(1,128)S(1)}, f32[8,1,256,4,1,256]{5,4,3,2,1,0:T(1,128)}, u32[]{:S(2)}) %copy-start) | copy-done | bytes 8388632
  258.0 0.0 copy-start.1
  258.0 1.6 copy-done.1
  259.6 4.9 %merge.1 = f32[16384,128]{1,0:T(8,128)} custom-call(f32[16384,128]{1,0:T(8,128)S(1)} %bitcast.4, f32[4096,128]{1,0:T(8,128)S(1)} %copy-done.1), custom_call_target="tpu_custom_call" | custom-call | tf_op jit(solution)/shard_map/merge/pallas_call | solution.py:815
Async XLA Ops:
  254.6 3.4 %copy-start = (f32[8,1,256,4,1,256]{5,4,3,2,1,0:T(1,128)S(1)}, f32[8,1,256,4,1,256]{5,4,3,2,1,0:T(1,128)}, u32[]{:S(2)}) copy-start(f32[8,1,256,4,1,256]{5,4,3,2,1,0:T(1,128)} %param.3) | copy-start | bytes 25165828
  258.0 1.6 copy-start.1

commit v2 on v1

--- a/solution.py
+++ b/solution.py
@@ -75,10 +75,11 @@
 
 
 def sweep_kernel(
-    panel,
+    factor,
     adj,
     out,
     s_ref,
+    panel,
     crow,
     ccol,
     ct,
@@ -98,11 +99,13 @@
     apiece,
     qbuf,
     qinv,
-    tbuf,
-    trecv,
+    tpart,
+    tin1,
+    tsum,
+    tin2,
     tslice,
-    tall1,
-    tall0,
+    tin3,
+    tall,
     rblk,
     rsend,
     done,
@@ -121,10 +124,10 @@
     moved_sem,
     ga_s,
     ga_r,
-    t_s,
-    t_r,
-    root_s,
-    root_r,
+    t1,
+    t2,
+    t3,
+    troot,
     blk_sem,
 ):
     r, c = lax.axis_index("row"), lax.axis_index("col")
@@ -165,8 +168,12 @@
             src_ref=src, dst_ref=src, send_sem=ss, recv_sem=ss, device_id=mate, device_id_type=MESH
         ).wait_send()
 
+    holds_panel = c < 2
     load = pltpu.make_async_copy(adj, s_ref, local_sem.at[0])
-    load.start()
+
+    @pl.when(holds_panel)
+    def _():
+        pltpu.make_async_copy(factor, s_ref, local_sem.at[1]).start()
 
     barrier = pltpu.get_barrier_semaphore()
 
@@ -180,7 +187,9 @@
     away = jnp.logical_or(target[0] != r, target[1] != c)
     from_away = jnp.logical_or(giver[0] != r, giver[1] != c)
     is_root = jnp.logical_and(r == 0, c == 0)
-    owes_root = jnp.logical_and(r > 0, c == 1)
+    owes_root = jnp.logical_and(r > 0, jnp.logical_and(c > 0, c < 4))
+    at_11 = jnp.logical_and(r == 1, c == 1)
+    at_10 = jnp.logical_and(r == 1, c == 0)
 
     @pl.when(from_away)
     def _():
@@ -189,9 +198,29 @@
     @pl.when(is_root)
     def _():
         for step in range(1, 8):
-            greet((step, 1))
-
-    pl.semaphore_wait(barrier, 22 + jnp.where(away, 1, 0) + jnp.where(owes_root, 1, 0))
+            for other in range(1, 4):
+                greet((step, other))
+
+    @pl.when(at_11)
+    def _():
+        greet((0, 0))
+
+    @pl.when(holds_panel)
+    def _():
+        pltpu.make_async_copy(factor, s_ref, local_sem.at[1]).wait()
+
+        def take(k, carry):
+            for h in range(2):
+                panel[k, :, pl.ds(128 * h, 128)] = s_ref[pl.ds(k * 1024 + h, 128, stride=8), :]
+            return carry
+
+        lax.fori_loop(0, 16, take, 0)
+
+    load.start()
+    pl.semaphore_wait(
+        barrier,
+        22 + jnp.where(away, 1, 0) + jnp.where(owes_root, 1, 0) + jnp.where(is_root, 1, 0),
+    )
 
     order = (10, 11, 14, 15, 6, 7, 8, 9, 12, 13, 2, 3, 5, 4, 1, 0)
     for p in range(2):
@@ -284,15 +313,34 @@
             send(src, ccol.at[p, b], chain_s.at[p, b, 1], chain_r.at[p, b], mate)
             pltpu.make_async_copy(src, ccol.at[p, b], local_sem.at[2 + p * 4 + b]).start()
 
-    def relay(p, b):
+    even = gap[0] == 2
+    near = jnp.where(gap[0] == 3, 1, 0)
+    turns = (
+        ((0, 0), (0, 0)),
+        ((0, 1), (1, 0)),
+        ((0, 2), (0, 1)),
+        ((1, 0), (1, 1)),
+        ((0, 3), (0, 2)),
+        ((1, 1), (1, 2)),
+        ((1, 2), (0, 3)),
+        ((1, 3), (1, 3)),
+    )
+
+    def relay(step):
+        (side, b), (even_side, even_b) = turns[step]
+        p = jnp.where(even, even_side, jnp.where(near == 1, 1 - side, side))
+        b = jnp.where(even, even_b, b)
+        distance = jnp.where(p == 0, gap[0], gap[1])
+        onward = jnp.where(p == 0, next_y[0], next_y[1])
+
         @pl.when(relays)
         def _():
             held = ccol.at[p, b]
             arrived(held, chain_r.at[p, b])
 
-            @pl.when(gap[p] < 3)
+            @pl.when(distance < 3)
             def _():
-                send(held, held, chain_s.at[p, b, 0], chain_r.at[p, b], (next_y[p] * 2 + core, c))
+                send(held, held, chain_s.at[p, b, 0], chain_r.at[p, b], (onward * 2 + core, c))
 
             send(held, held, chain_s.at[p, b, 1], chain_r.at[p, b], mate)
 
@@ -315,9 +363,6 @@
         return jnp.concatenate(
             [s_ref[pl.ds(a * 2048 + 2 * b + h, 256, stride=8), :] for h in range(2)], axis=1
         )
-
-    at_11 = jnp.logical_and(r == 1, c == 1)
-    at_10 = jnp.logical_and(r == 1, c == 0)
 
     @pl.when(at_11)
     def _():
@@ -361,9 +406,9 @@
 
         lax.fori_loop(0, 4, per_block, 0)
 
-    for step, (p, b) in enumerate(chunks):
+    for step in range(8):
         mirrored(step)
-        relay(p, b)
+        relay(step)
 
     for b in range(4):
         post(
@@ -557,89 +602,88 @@
         def _():
             send(apiece.at[p], agath.at[c], ga_s.at[p], ga_r.at[c], (r, p))
 
-    hand_in(1)
     solved_0 = exact(sums_0 - exact(solved_1, pivot(1)), qinv[0])
     apiece[0] = solved_0
+
+    sides_1, sides_0 = [tuple(v.T for v in split(m)) for m in (solved_1, solved_0)]
+    right_1, right_0 = split(crow[1, c]), split(crow[0, c])
+    for n, term in enumerate((dot3(sides_1, right_1), dot3(sides_1, right_0), dot3(sides_0, right_0))):
+        for t in range(8):
+            tpart[t, n] = term[32 * t : 32 * t + 32]
+    for step in range(1, 8):
+        to = lax.rem(r + step, 8)
+        post(tpart.at[to], tin1.at[step], t1.at[0, step], t1.at[1, step], (to, c))
+    hand_in(1)
     hand_in(0)
-
-    @pl.when(c < 2)
-    def _():
-        for p in range(2):
-
-            @pl.when(c == p)
-            def _():
-                agath[p] = apiece[p]
-
-                for k in range(16):
-                    if k != p:
-                        arrived(agath.at[k], ga_r.at[k])
-
-        def gathered(k, total):
-            high, low = split(agath[k])
-            sides = (high.T, low.T)
-            first = dot3(sides, split(crow[c, k]))
-            second = dot3(sides, split(crow[0, k]))
-            return total[0] + first, total[1] + second
-
-        zero = jnp.zeros((256, 256), F32)
-        total = lax.fori_loop(0, 16, gathered, (zero, zero))
-        for t in range(8):
-            for n in range(2):
-                tbuf[t, n] = total[n][32 * t : 32 * t + 32]
-        for step in range(1, 8):
-            to = lax.rem(r + step, 8)
-            send(tbuf.at[to], trecv.at[step], t_s.at[step], t_r.at[step], (to, c))
-        result = tbuf[r]
-        for step in range(1, 8):
-            arrived(trecv.at[step], t_r.at[step])
-            result = result + trecv[step]
-        tslice[...] = result
-
-        @pl.when(c == 1)
-        def _():
-            send(tslice, tall1.at[r], root_s.at[0], root_r.at[0, r], (0, 0))
-
-            @pl.when(r != 1)
-            def _():
-                send(tslice, tall1.at[r], root_s.at[1], root_r.at[0, r], (1, 1))
-
-        @pl.when(jnp.logical_and(c == 0, r != 0))
-        def _():
-            send(tslice.at[0], tall0.at[r], root_s.at[0], root_r.at[1, r], (0, 0))
+    result = tpart[r]
+    for step in range(1, 8):
+        arrived(tin1.at[step], t1.at[1, step])
+        result = result + tin1[step]
+    for t in range(4):
+        tsum[t] = result[:, 8 * t : 8 * t + 8]
+    for step in range(1, 4):
+        to = lax.rem(x + step, 4)
+        post(tsum.at[to], tin2.at[step], t2.at[0, step], t2.at[1, step], (r, 4 * z + to))
+    result = tsum[x]
+    for step in range(1, 4):
+        arrived(tin2.at[step], t2.at[1, step])
+        result = result + tin2[step]
+    tslice[...] = result
+
+    @pl.when(z != 0)
+    def _():
+        send(tslice, tin3.at[z], t3.at[0], t3.at[z], (r, x))
+
+    @pl.when(z == 0)
+    def _():
+        total = result
+        for n in range(1, 4):
+            arrived(tin3.at[n], t3.at[n])
+            total = total + tin3[n]
+        tslice[...] = total
+
+        @pl.when(jnp.logical_not(is_root))
+        def _():
+            send(tslice, tall.at[r, x], t3.at[0], troot.at[r, x], (0, 0))
 
     def flat(parts):
         return jnp.concatenate(parts, axis=0)
 
-    @pl.when(at_11)
-    def _():
-        tall1[1] = tslice[...]
+    @pl.when(is_root)
+    def _():
+        tall[0, 0] = tslice[...]
         for t in range(8):
-            if t != 1:
-                arrived(tall1.at[t], root_r.at[0, t])
-        sums = flat([tall1[t, 0] for t in range(8)])
-        done[...] = diag_step(pivot(2), qinv[1], lower(adjoint_block(0, 0) - sums))
-
-    @pl.when(is_root)
-    def _():
-        tall0[0] = tslice[0]
-        for t in range(8):
-            arrived(tall1.at[t], root_r.at[0, t])
+            for n in range(4):
+                if t + n > 0:
+                    arrived(tall.at[t, n], troot.at[t, n])
         arrived(rblk.at[0], blk_sem.at[2])
         arrived(rblk.at[1], blk_sem.at[3])
-        sums = flat([tall1[t, 0] for t in range(8)])
-        diag_1 = diag_step(pivot(2), qinv[1], lower(rblk[0] - sums))
-        cross = flat([tall1[t, 1] for t in range(8)])
+
+        def total(n):
+            return flat([tall[t, m, n] for t in range(8) for m in range(4)])
+
+        diag_1 = diag_step(pivot(2), qinv[1], lower(rblk[0] - total(0)))
+        rblk[0] = diag_1
+        send(rblk.at[0], a01, blk_sem.at[6], blk_sem.at[5], (1, 1))
         link = pivot(1)
-        rows_1 = exact(rblk[1] - cross - exact(diag_1 + diag_1.T, link), qinv[0])
+        rows_1 = exact(rblk[1] - total(1) - exact(diag_1 + diag_1.T, link), qinv[0])
         rsend[...] = rows_1
         send(rsend, a01, blk_sem.at[4], blk_sem.at[5], (1, 0))
-        for t in range(1, 8):
-            arrived(tall0.at[t], root_r.at[1, t])
-        sums = flat([tall0[t] for t in range(8)]) + exact(rows_1.T, link)
+        sums = total(2) + exact(rows_1.T, link)
         done[...] = diag_step(pivot(0), qinv[0], lower(adjoint_block(0, 0) - sums))
         left(rsend, blk_sem.at[4])
-
-    @pl.when(at_10)
+        left(rblk.at[0], blk_sem.at[6])
+
+    for p in range(2):
+
+        @pl.when(c == p)
+        def _():
+            agath[p] = apiece[p]
+            for k in range(16):
+                if k != p:
+                    arrived(agath.at[k], ga_r.at[k])
+
+    @pl.when(jnp.logical_or(at_10, at_11))
     def _():
         arrived(a01, blk_sem.at[5])
         done[...] = a01[...]
@@ -711,25 +755,12 @@
     def _():
         left(moved, moved_sem.at[0])
 
-    @pl.when(c < 2)
-    def _():
-        for step in range(1, 8):
-            left(trecv.at[step], t_s.at[step])
-
-        @pl.when(c == 1)
-        def _():
-            left(tslice, root_s.at[0])
-
-            @pl.when(r != 1)
-            def _():
-                left(tslice, root_s.at[1])
-
-        @pl.when(jnp.logical_and(c == 0, r != 0))
-        def _():
-            left(tslice.at[0], root_s.at[0])
-
-
-def sweep(panel, adj):
+    @pl.when(jnp.logical_not(is_root))
+    def _():
+        left(tslice, t3.at[0])
+
+
+def sweep(factor, adj):
     vmem = pltpu.VMEM
     dma = pltpu.SemaphoreType.DMA
     return pl.pallas_call(
@@ -739,6 +770,7 @@
         out_specs=pl.BlockSpec(memory_space=pltpu.VMEM),
         scratch_shapes=[
             vmem((16384, 128), F32),
+            vmem((16, 128, 256), F32),
             vmem((2, 16, 128, 256), F32),
             vmem((2, 4, 2, 128, 256), F32),
             vmem((2, 512, 256), BF16),
@@ -758,11 +790,13 @@
             vmem((2, 128, 256), F32),
             vmem((3, 2, 128, 256), F32),
             vmem((2, 256, 256), F32),
-            vmem((8, 2, 32, 256), F32),
-            vmem((8, 2, 32, 256), F32),
-            vmem((2, 32, 256), F32),
-            vmem((8, 2, 32, 256), F32),
-            vmem((8, 32, 256), F32),
+            vmem((8, 3, 32, 256), F32),
+            vmem((8, 3, 32, 256), F32),
+            vmem((4, 3, 8, 256), F32),
+            vmem((4, 3, 8, 256), F32),
+            vmem((3, 8, 256), F32),
+            vmem((4, 3, 8, 256), F32),
+            vmem((8, 4, 3, 8, 256), F32),
             vmem((2, 256, 256), F32),
             vmem((256, 256), F32),
             vmem((256, 256), F32),
@@ -781,17 +815,17 @@
             dma((2,)),
             dma((2,)),
             dma((16,)),
-            dma((8,)),
-            dma((8,)),
-            dma((2,)),
             dma((2, 8)),
-            dma((6,)),
+            dma((2, 4)),
+            dma((4,)),
+            dma((8, 4)),
+            dma((7,)),
         ],
         compiler_params=pltpu.CompilerParams(
             collective_id=0, has_side_effects=True, vmem_limit_bytes=60 * 2**20
         ),
         name="sweep",
-    )(panel, adj)
+    )(factor, adj)
 
 
 def merge_kernel(adj, panel, out):
@@ -821,15 +855,14 @@
             pl.BlockSpec((512, 128), lambda a: (a, 0)),
         ],
         out_specs=pl.BlockSpec((2048, 128), lambda a: (a, 0)),
-        compiler_params=pltpu.CompilerParams(vmem_limit_bytes=32 * 2**20),
+        compiler_params=pltpu.CompilerParams(vmem_limit_bytes=60 * 2**20),
         name="merge",
     )(adj, panel)
 
 
 def shards(factor, adjoint):
-    panel = factor[:, 0, :, 0, 0, :].reshape(16, 128, 256)
     adj = adjoint.reshape(16384, 128)
-    solved = sweep(panel, adj)
+    solved = sweep(factor.reshape(16384, 128), adj)
     return merge(adj, solved).reshape(adjoint.shape)
 
 

time: 269 us -> 188 us (0.70); the launches traced: 265 us -> 188 us
  Pallas kernels: 255 us -> 188 us
  local copies, waits for them, and re-layouts: 9.55 us -> 0 us
    pallas_call x1, Pallas kernels: 250 us -> 178 us  [sweep(): pl.pallas_call(sweep_kernel, out_shape=jax.ShapeDtypeStruct((4096, 128),...]
    unnamed x5 -> x0, local copies, waits for them, and re-layouts: 6.52 us -> none
    pallas_call x1, Pallas kernels: 4.95 us -> 9.6 us  [merge(): pl.pallas_call(merge_kernel, grid=(8,), out_shape=jax.ShapeDtypeStruct((1...]
    slice x1 -> x0, local copies, waits for them, and re-layouts: 3.03 us -> none  [shards(): panel = factor[:, 0, :, 0, 0, :].reshape(16, 128, 256)]
where the time goes in v2:
time: 188 us
  Pallas kernels  188 us (100%)
    pallas_call x1, Pallas kernels, sweep(): pl.pallas_call(sweep_kernel, out_shape=jax.ShapeDtypeStruct((4096, 128),...  178 us
    pallas_call x1, Pallas kernels, merge(): pl.pallas_call(merge_kernel, grid=(8,), out_shape=jax.ShapeDtypeStruct((1...  9.6 us

profile of v2, /device:TPU:3, one launch (start us, length us, event | category | flops | bytes accessed | tf_op | source)
XLA Modules:
  0.0 188.1 jit_solution(10779329010664931663)
XLA Ops:
  0.0 178.4 %sweep.1.panel = f32[4096,128]{1,0:T(8,128)} custom-call(f32[16384,128]{1,0:T(8,128)} %bitcast.5, f32[16384,128]{1,0:T(8,128)} %bitcast.3), custom_call_target="tpu_custom_call" | custom-call | tf_op jit(solution)/shard_map/sweep/pallas_call | solution.py:766
  178.5 9.6 %merge.1 = f32[16384,128]{1,0:T(8,128)} custom-call(f32[16384,128]{1,0:T(8,128)} %bitcast.4, f32[4096,128]{1,0:T(8,128)} %sweep.1.panel), custom_call_target="tpu_custom_call" | custom-call | tf_op jit(solution)/shard_map/merge/pallas_call | solution.py:849

commit v3 on v2

--- a/solution.py
+++ b/solution.py
@@ -8,6 +8,7 @@
 F32, BF16 = jnp.float32, jnp.bfloat16
 MESH = pl.DeviceIdType.MESH
 precise = lax.Precision.HIGHEST
+WAVES = 1
 
 
 def up(v):
@@ -69,9 +70,17 @@
     return found
 
 
+def times(left, right):
+    return dot3(left if isinstance(left, tuple) else split(left), right if isinstance(right, tuple) else split(right))
+
+
+def turned(parts):
+    return tuple(part.T for part in parts)
+
+
 def diag_step(pivot, inverse, target):
-    inner = halve_diag(exact(pivot.T, target))
-    return halve_diag(exact(exact(inverse.T, inner), inverse))
+    inner = halve_diag(times(pivot, target))
+    return halve_diag(times(times(turned(inverse), inner), inverse))
 
 
 def sweep_kernel(
@@ -82,6 +91,7 @@
     panel,
     crow,
     ccol,
+    stage,
     ct,
     sw,
     cc,
@@ -93,8 +103,7 @@
     moved,
     opp1,
     nbr1,
-    opp2,
-    nbr2,
+    near,
     agath,
     apiece,
     qbuf,
@@ -115,11 +124,13 @@
     scat_r,
     ag1,
     ag2,
-    chain_s,
-    chain_r,
+    stage_s,
+    stage_r,
+    col_sem,
     q_s,
     q_r,
     ring,
+    ring2,
     mate_sem,
     moved_sem,
     ga_s,
@@ -195,6 +206,10 @@
     def _():
         greet(giver)
 
+    @pl.when(away)
+    def _():
+        greet(target)
+
     @pl.when(is_root)
     def _():
         for step in range(1, 8):
@@ -219,130 +234,193 @@
     load.start()
     pl.semaphore_wait(
         barrier,
-        22 + jnp.where(away, 1, 0) + jnp.where(owes_root, 1, 0) + jnp.where(is_root, 1, 0),
+        22
+        + jnp.where(away, 1, 0)
+        + jnp.where(from_away, 1, 0)
+        + jnp.where(owes_root, 1, 0)
+        + jnp.where(is_root, 1, 0),
     )
 
-    order = (10, 11, 14, 15, 6, 7, 8, 9, 12, 13, 2, 3, 5, 4, 1, 0)
+    orders = (
+        (9, 10, 15, 8, 11, 7, 6, 14, 2, 5, 13, 3, 4, 12, 1),
+        (8, 11, 14, 9, 10, 6, 7, 15, 3, 4, 12, 2, 5, 13, 0),
+    )
+    groups = (
+        {4: (9, 8, 6, 5), 12: (10, 11, 14, 13), 3: (15, 7, 2)},
+        {5: (8, 9, 7, 4), 13: (11, 10, 15, 12), 2: (14, 6, 3)},
+    )
+    relays = [
+        {k: (via, slot) for via, members in g.items() for slot, k in enumerate(members)} for g in groups
+    ]
+    rows = 128 // WAVES
+
+    def wave(ref, w):
+        return ref.at[pl.ds(rows * w, rows)]
+
+    for w in range(WAVES):
+        for p in range(2):
+
+            @pl.when(c == p)
+            def _():
+                for k in orders[p]:
+                    src = wave(panel.at[k], w)
+                    if k in relays[p]:
+                        via, slot = relays[p][k]
+                        send(src, stage.at[slot, w], scat_s.at[k, w], stage_r.at[slot, w], (r, via))
+                    else:
+                        send(src, wave(crow.at[p, k], w), scat_s.at[k, w], scat_r.at[p, w], (r, k))
+
     for p in range(2):
 
         @pl.when(c == p)
         def _():
-            for k in order:
-                if k != p:
-                    send(panel.at[k], crow.at[p, k], scat_s.at[k], scat_r.at[p], (r, k))
             own = pltpu.make_async_copy(panel.at[p], crow.at[p, p], local_sem.at[1])
             own.start()
             own.wait()
 
-    def halves(ref, half):
-        return ref.at[pl.ds(64 * half, 64)]
-
-    def gather_second(p, q, first):
+    def pass_on(w):
+        for p in range(2):
+            for via, members in groups[p].items():
+
+                @pl.when(c == via)
+                def _():
+                    for slot, k in enumerate(members):
+                        held = stage.at[slot, w]
+                        arrived(held, stage_r.at[slot, w])
+                        send(held, wave(crow.at[p, k], w), stage_s.at[slot, w], scat_r.at[p, w], (r, k))
+
+    def quarter(p, k, w, half):
+        return crow.at[p, k, pl.ds(rows * w + rows // 2 * half, rows // 2)]
+
+    def gather_second(p, w, q, first):
         f, s = place[p]
-        held = crow.at[p, piece(p, first, s)]
-        post(held, held, ag2.at[0, p, q, 0], ag2.at[1, p, q, 0], member(p, f, up(s)))
-        post(held, held, ag2.at[0, p, q, 1], ag2.at[1, p, q, 1], member(p, f, down(s)))
-
-    for p in range(2):
-        f, s = place[p]
-        held = crow.at[p, piece(p, f, s)]
-
-        @pl.when(c != p)
-        def _():
-            arrived(crow.at[p, c], scat_r.at[p])
-
-        post(held, held, ag1.at[0, p, 0], ag1.at[1, p, 0], member(p, up(f), s))
-        post(held, held, ag1.at[0, p, 1], ag1.at[1, p, 1], member(p, down(f), s))
-        gather_second(p, 0, f)
-    for p in range(2):
-        f, s = place[p]
-        held = crow.at[p, piece(p, down(f), s)]
-        arrived(held, ag1.at[1, p, 0])
-        part = halves(held, 0)
-        post(part, part, ag1.at[0, p, 2], ag1.at[1, p, 2], member(p, up(f), s))
-        gather_second(p, 1, down(f))
-        held = crow.at[p, piece(p, up(f), s)]
-        arrived(held, ag1.at[1, p, 1])
-        part = halves(held, 1)
-        post(part, part, ag1.at[0, p, 3], ag1.at[1, p, 3], member(p, down(f), s))
-        gather_second(p, 2, up(f))
-    for p in range(2):
-        f, s = place[p]
-        held = crow.at[p, piece(p, across_from(f), s)]
-        arrived(halves(held, 0), ag1.at[1, p, 2])
-        arrived(halves(held, 1), ag1.at[1, p, 3])
-        gather_second(p, 3, across_from(f))
-    for q in range(4):
+        held = wave(crow.at[p, piece(p, first, s)], w)
+        post(held, held, ag2.at[0, w, p, q, 0], ag2.at[1, w, p, q, 0], member(p, f, up(s)))
+        post(held, held, ag2.at[0, w, p, q, 1], ag2.at[1, w, p, q, 1], member(p, f, down(s)))
+
+    def gather_open(w):
         for p in range(2):
             f, s = place[p]
-            first = (f, down(f), up(f), across_from(f))[q]
-            held = crow.at[p, piece(p, first, down(s))]
-            arrived(held, ag2.at[1, p, q, 0])
-            part = halves(held, 0)
-            post(part, part, ag2.at[0, p, q, 2], ag2.at[1, p, q, 2], member(p, f, up(s)))
-            held = crow.at[p, piece(p, first, up(s))]
-            arrived(held, ag2.at[1, p, q, 1])
-            part = halves(held, 1)
-            post(part, part, ag2.at[0, p, q, 3], ag2.at[1, p, q, 3], member(p, f, down(s)))
-    for q in range(4):
+            held = wave(crow.at[p, piece(p, f, s)], w)
+
+            @pl.when(c != p)
+            def _():
+                arrived(wave(crow.at[p, c], w), scat_r.at[p, w])
+
+            post(held, held, ag1.at[0, w, p, 0], ag1.at[1, w, p, 0], member(p, up(f), s))
+            post(held, held, ag1.at[0, w, p, 1], ag1.at[1, w, p, 1], member(p, down(f), s))
+            gather_second(p, w, 0, f)
+
+    def gather_first(w):
         for p in range(2):
             f, s = place[p]
-            first = (f, down(f), up(f), across_from(f))[q]
-            held = crow.at[p, piece(p, first, across_from(s))]
-            arrived(halves(held, 0), ag2.at[1, p, q, 2])
-            arrived(halves(held, 1), ag2.at[1, p, q, 3])
+            k = piece(p, down(f), s)
+            arrived(wave(crow.at[p, k], w), ag1.at[1, w, p, 0])
+            part = quarter(p, k, w, 0)
+            post(part, part, ag1.at[0, w, p, 2], ag1.at[1, w, p, 2], member(p, up(f), s))
+            gather_second(p, w, 1, down(f))
+            k = piece(p, up(f), s)
+            arrived(wave(crow.at[p, k], w), ag1.at[1, w, p, 1])
+            part = quarter(p, k, w, 1)
+            post(part, part, ag1.at[0, w, p, 3], ag1.at[1, w, p, 3], member(p, down(f), s))
+            gather_second(p, w, 2, up(f))
+        for p in range(2):
+            f, s = place[p]
+            k = piece(p, across_from(f), s)
+            arrived(quarter(p, k, w, 0), ag1.at[1, w, p, 2])
+            arrived(quarter(p, k, w, 1), ag1.at[1, w, p, 3])
+            gather_second(p, w, 3, across_from(f))
+
+    def firsts(f):
+        return f, down(f), up(f), across_from(f)
+
+    def gather_relay(w, q):
+        for p in range(2):
+            f, s = place[p]
+            first = firsts(f)[q]
+            k = piece(p, first, down(s))
+            arrived(wave(crow.at[p, k], w), ag2.at[1, w, p, q, 0])
+            part = quarter(p, k, w, 0)
+            post(part, part, ag2.at[0, w, p, q, 2], ag2.at[1, w, p, q, 2], member(p, f, up(s)))
+            k = piece(p, first, up(s))
+            arrived(wave(crow.at[p, k], w), ag2.at[1, w, p, q, 1])
+            part = quarter(p, k, w, 1)
+            post(part, part, ag2.at[0, w, p, q, 3], ag2.at[1, w, p, q, 3], member(p, f, down(s)))
+
+    def gather_close(w):
+        for q in range(4):
+            for p in range(2):
+                f, s = place[p]
+                k = piece(p, firsts(f)[q], across_from(s))
+                arrived(quarter(p, k, w, 0), ag2.at[1, w, p, q, 2])
+                arrived(quarter(p, k, w, 1), ag2.at[1, w, p, q, 3])
+
+    here = ccol.at[y, core]
+
+    def to_mate(n, slot):
+        post(slot, slot, col_sem.at[0, n], col_sem.at[1, n], mate)
+
+    def column_send():
+        own = crow.at[:, c]
+
+        @pl.when(from_away)
+        def _():
+            send(own, ccol.at[z, lax.rem(x, 2)], col_sem.at[0, 0], col_sem.at[1, 0], giver)
+
+        @pl.when(jnp.logical_not(from_away))
+        def _():
+            copy = pltpu.make_async_copy(own, here, local_sem.at[1])
+            copy.start()
+            copy.wait()
+
+    def column_open():
+        @pl.when(away)
+        def _():
+            arrived(here, col_sem.at[1, 0])
+
+        post(here, here, col_sem.at[0, 1], col_sem.at[1, 1], (up(y) * 2 + core, c))
+        post(here, here, col_sem.at[0, 2], col_sem.at[1, 2], (down(y) * 2 + core, c))
+        to_mate(5, here)
+
+    def column_relay():
+        slot = ccol.at[down(y), core]
+        arrived(slot, col_sem.at[1, 1])
+        post(slot.at[0], slot.at[0], col_sem.at[0, 3], col_sem.at[1, 3], (up(y) * 2 + core, c))
+        to_mate(6, slot)
+        slot = ccol.at[up(y), core]
+        arrived(slot, col_sem.at[1, 2])
+        post(slot.at[1], slot.at[1], col_sem.at[0, 4], col_sem.at[1, 4], (down(y) * 2 + core, c))
+        to_mate(7, slot)
+
+    def column_close():
+        slot = ccol.at[across_from(y), core]
+        arrived(slot.at[0], col_sem.at[1, 3])
+        arrived(slot.at[1], col_sem.at[1, 4])
+        to_mate(8, slot)
+
+    def column_wait():
+        for n, t in ((5, y), (6, down(y)), (7, up(y)), (8, across_from(y))):
+            arrived(ccol.at[t, 1 - core], col_sem.at[1, n])
+
+    for w in range(WAVES):
+        pass_on(w)
+        gather_open(w)
+    column_send()
+    for w in range(WAVES):
+        gather_first(w)
+    column_open()
+    for w in range(WAVES):
+        gather_relay(w, 0)
+        gather_relay(w, 1)
+    column_relay()
+    for w in range(WAVES):
+        gather_relay(w, 2)
+        gather_relay(w, 3)
+    column_close()
+    for w in range(WAVES):
+        gather_close(w)
 
     load.wait()
-
-    in_line = core == home_core
-    is_home = jnp.logical_and(in_line, y == home_y)
-    relays = jnp.logical_and(in_line, y != home_y)
-    next_y = (up(y), down(y))
-    gap = (lax.rem(y - home_y + 4, 4), lax.rem(home_y - y + 4, 4))
-
-    def home_pieces(p, b):
-        return crow.at[p, pl.ds(4 * b + 2 * group, 2)]
-
-    chunks = [(p, b) for b in range(4) for p in range(2)]
-
-    @pl.when(is_home)
-    def _():
-        for p, b in chunks:
-            src = home_pieces(p, b)
-            send(src, ccol.at[p, b], chain_s.at[p, b, 0], chain_r.at[p, b], (next_y[p] * 2 + core, c))
-            send(src, ccol.at[p, b], chain_s.at[p, b, 1], chain_r.at[p, b], mate)
-            pltpu.make_async_copy(src, ccol.at[p, b], local_sem.at[2 + p * 4 + b]).start()
-
-    even = gap[0] == 2
-    near = jnp.where(gap[0] == 3, 1, 0)
-    turns = (
-        ((0, 0), (0, 0)),
-        ((0, 1), (1, 0)),
-        ((0, 2), (0, 1)),
-        ((1, 0), (1, 1)),
-        ((0, 3), (0, 2)),
-        ((1, 1), (1, 2)),
-        ((1, 2), (0, 3)),
-        ((1, 3), (1, 3)),
-    )
-
-    def relay(step):
-        (side, b), (even_side, even_b) = turns[step]
-        p = jnp.where(even, even_side, jnp.where(near == 1, 1 - side, side))
-        b = jnp.where(even, even_b, b)
-        distance = jnp.where(p == 0, gap[0], gap[1])
-        onward = jnp.where(p == 0, next_y[0], next_y[1])
-
-        @pl.when(relays)
-        def _():
-            held = ccol.at[p, b]
-            arrived(held, chain_r.at[p, b])
-
-            @pl.when(distance < 3)
-            def _():
-                send(held, held, chain_s.at[p, b, 0], chain_r.at[p, b], (onward * 2 + core, c))
-
-            send(held, held, chain_s.at[p, b, 1], chain_r.at[p, b], mate)
 
     pivots = ((0, 0, 0), (1, 0, 1), (2, 1, 1))
 
@@ -408,27 +486,18 @@
 
     for step in range(8):
         mirrored(step)
-        relay(step)
 
     for b in range(4):
         post(
             macc.at[b, 1 - core], mate_in.at[b], mate_sem.at[0, b], mate_sem.at[1, b], mate
         )
 
-    @pl.when(is_home)
-    def _():
-        for p, b in chunks:
-            pltpu.make_async_copy(home_pieces(p, b), ccol.at[p, b], local_sem.at[2 + p * 4 + b]).wait()
-
-    @pl.when(jnp.logical_not(in_line))
-    def _():
-        for p, b in chunks:
-            arrived(ccol.at[p, b], chain_r.at[p, b])
+    column_wait()
 
     def ready_columns(b, carry):
         for p in range(2):
             for half in range(2):
-                high, low = split(ccol[p, b, half])
+                high, low = split(ccol[b, half, p])
                 rows, lanes = pl.ds(128 * half, 128), pl.ds(256 * p, 256)
                 cc[0, b, rows, lanes] = high
                 cc[1, b, rows, lanes] = low
@@ -460,20 +529,22 @@
         lax.fori_loop(0, 4, per_block, 0)
         return carry
 
-    lax.fori_loop(0, 8, direct, 0)
-
-    def ring_open(slot, held, pos, device, rows, opp, nbr):
+
+    def ring_open(slot, held, pos, device, rows, opp, nbr, stage=None):
         def part(ref, half):
             return ref.at[pl.ds(rows * half, rows)]
 
         def go(src, dst, n, where):
             post(src, dst, ring.at[0, slot, n], ring.at[1, slot, n], device(where))
 
-        far = held(across_from(pos))
-        go(part(far, 0), opp.at[0], 0, down(pos))
-        go(part(far, 1), opp.at[1], 1, up(pos))
-        go(part(held(down(pos)), 1), part(nbr.at[0], 1), 2, down(pos))
-        go(part(held(up(pos)), 0), part(nbr.at[1], 0), 3, up(pos))
+        if stage in (None, 0):
+            far = held(across_from(pos))
+            go(part(far, 0), opp.at[0], 0, down(pos))
+            go(part(far, 1), opp.at[1], 1, up(pos))
+        if stage in (None, 1):
+            go(part(held(up(pos)), 0), part(nbr.at[1], 0), 3, up(pos))
+        if stage in (None, 2):
+            go(part(held(down(pos)), 1), part(nbr.at[0], 1), 2, down(pos))
 
     def ring_pass(slot, held, pos, device, rows, opp, nbr):
         def part(ref, half):
@@ -514,17 +585,22 @@
             nbr1.at[p, j],
         )
 
-    def second_ring(p):
+    def second_open(p):
         f, s = place[p]
-        return (
-            8 + p,
-            lambda t: oacc.at[p, piece(p, t, s)],
-            f,
-            lambda t: member(p, t, s),
-            64,
-            opp2.at[p],
-            nbr2.at[p],
-        )
+        for n, hop in enumerate((across_from, up, down)):
+            to = hop(f)
+            post(
+                oacc.at[p, piece(p, to, s)],
+                near.at[p, n],
+                ring2.at[0, p, n],
+                ring2.at[1, p, n],
+                member(p, to, s),
+            )
+
+    def second_close(p):
+        for n in range(3):
+            arrived(near.at[p, n], ring2.at[1, p, n])
+        return oacc[p, c] + (near[p, 0] + (near[p, 1] + near[p, 2]))
 
     column_ring = (
         10,
@@ -535,9 +611,14 @@
         yopp,
         ynbr,
     )
-    rings = [first_ring(p, j) for j in range(4) for p in range(2)]
-    for spec in rings:
-        ring_open(*spec)
+    groups_of_rows = (across_from(z), up(z), down(z), z)
+    for n, owner in enumerate(groups_of_rows):
+        lax.fori_loop(2 * owner, 2 * owner + 2, direct, 0)
+        ring_open(*first_ring(1, owner))
+        if n < 3:
+            for j in range(4):
+                ring_open(*first_ring(0, j), stage=n)
+    rings = [ring for n in range(4) for ring in (first_ring(0, n), first_ring(1, groups_of_rows[n]))]
 
     for b in range(4):
         arrived(mate_in.at[b], mate_sem.at[1, b])
@@ -570,7 +651,7 @@
     for spec in rings:
         ring_close(*spec)
     for p in range(2):
-        ring_open(*second_ring(p))
+        second_open(p)
     ring_close(*column_ring)
 
     @pl.when(away)
@@ -581,10 +662,7 @@
     def _():
         moved[...] = macc[y, core]
 
-    for p in range(2):
-        ring_pass(*second_ring(p))
-    for p in range(2):
-        ring_close(*second_ring(p))
+    closed_0, closed_1 = second_close(0), second_close(1)
 
     @pl.when(from_away)
     def _():
@@ -592,9 +670,10 @@
 
     keep = jnp.where(jnp.logical_and(c < 2, r < 2), 0.0, -1.0)
     extra = moved[...].T
-    sums_1 = (oacc[1, c] + extra[:, 256:]) * keep
-    sums_0 = (oacc[0, c] + extra[:, :256]) * keep
-    solved_1 = exact(sums_1, qinv[1])
+    sums_1 = (closed_1 + extra[:, 256:]) * keep
+    sums_0 = (closed_0 + extra[:, :256]) * keep
+    parts_1, parts_0 = split(qinv[1]), split(qinv[0])
+    solved_1 = times(sums_1, parts_1)
     apiece[1] = solved_1
 
     def hand_in(p):
@@ -602,7 +681,7 @@
         def _():
             send(apiece.at[p], agath.at[c], ga_s.at[p], ga_r.at[c], (r, p))
 
-    solved_0 = exact(sums_0 - exact(solved_1, pivot(1)), qinv[0])
+    solved_0 = times(sums_0 - times(solved_1, pivot(1)), parts_0)
     apiece[0] = solved_0
 
     sides_1, sides_0 = [tuple(v.T for v in split(m)) for m in (solved_1, solved_0)]
@@ -652,6 +731,9 @@
     @pl.when(is_root)
     def _():
         tall[0, 0] = tslice[...]
+        link = split(pivot(1))
+        pivot_1, pivot_0 = turned(split(pivot(2))), turned(split(pivot(0)))
+        ahead = split(times(link, parts_0))
         for t in range(8):
             for n in range(4):
                 if t + n > 0:
@@ -662,15 +744,14 @@
         def total(n):
             return flat([tall[t, m, n] for t in range(8) for m in range(4)])
 
-        diag_1 = diag_step(pivot(2), qinv[1], lower(rblk[0] - total(0)))
+        diag_1 = diag_step(pivot_1, parts_1, lower(rblk[0] - total(0)))
         rblk[0] = diag_1
         send(rblk.at[0], a01, blk_sem.at[6], blk_sem.at[5], (1, 1))
-        link = pivot(1)
-        rows_1 = exact(rblk[1] - total(1) - exact(diag_1 + diag_1.T, link), qinv[0])
+        rows_1 = times(rblk[1] - total(1), parts_0) - times(diag_1 + diag_1.T, ahead)
         rsend[...] = rows_1
         send(rsend, a01, blk_sem.at[4], blk_sem.at[5], (1, 0))
-        sums = total(2) + exact(rows_1.T, link)
-        done[...] = diag_step(pivot(0), qinv[0], lower(adjoint_block(0, 0) - sums))
+        sums = total(2) + times(turned(split(rows_1)), link)
+        done[...] = diag_step(pivot_0, parts_0, lower(adjoint_block(0, 0) - sums))
         left(rsend, blk_sem.at[4])
         left(rblk.at[0], blk_sem.at[6])
 
@@ -714,23 +795,24 @@
 
         @pl.when(c == p)
         def _():
-            for k in range(16):
-                if k != p:
-                    left(panel.at[k], scat_s.at[k])
+            for k in orders[p]:
+                for w in range(WAVES):
+                    left(wave(panel.at[k], w), scat_s.at[k, w])
 
         @pl.when(c != p)
         def _():
             left(apiece.at[p], ga_s.at[p])
 
-    for p, b in chunks:
-
-        @pl.when(in_line)
-        def _():
-            left(ccol.at[p, b], chain_s.at[p, b, 1])
-
-            @pl.when(gap[p] < 3)
+        for via, slot in relays[p].values():
+
+            @pl.when(c == via)
             def _():
-                left(ccol.at[p, b], chain_s.at[p, b, 0])
+                for w in range(WAVES):
+                    left(stage.at[slot, w], stage_s.at[slot, w])
+
+    @pl.when(from_away)
+    def _():
+        left(here, col_sem.at[0, 0])
 
     for slot, p, holder in pivots:
 
@@ -772,7 +854,8 @@
             vmem((16384, 128), F32),
             vmem((16, 128, 256), F32),
             vmem((2, 16, 128, 256), F32),
-            vmem((2, 4, 2, 128, 256), F32),
+            vmem((4, 2, 2, 128, 256), F32),
+            vmem((4, WAVES, 128 // WAVES, 256), F32),
             vmem((2, 512, 256), BF16),
             vmem((2, 8, 4, 256, 256), BF16),
             vmem((2, 4, 256, 512), BF16),
@@ -784,8 +867,7 @@
             vmem((512, 128), F32),
             vmem((2, 4, 2, 64, 256), F32),
             vmem((2, 4, 2, 128, 256), F32),
-            vmem((2, 2, 64, 256), F32),
-            vmem((2, 2, 128, 256), F32),
+            vmem((2, 3, 128, 256), F32),
             vmem((16, 128, 256), F32),
             vmem((2, 128, 256), F32),
             vmem((3, 2, 128, 256), F32),
@@ -802,15 +884,17 @@
             vmem((256, 256), F32),
             vmem((256, 256), F32),
             dma((10,)),
-            dma((16,)),
-            dma((2,)),
-            dma((2, 2, 4)),
-            dma((2, 2, 4, 4)),
-            dma((2, 4, 2)),
-            dma((2, 4)),
+            dma((16, WAVES)),
+            dma((2, WAVES)),
+            dma((2, WAVES, 2, 4)),
+            dma((2, WAVES, 2, 4, 4)),
+            dma((4, WAVES)),
+            dma((4, WAVES)),
+            dma((2, 9)),
             dma((3, 4)),
             dma((3,)),
             dma((2, 11, 6)),
+            dma((2, 2, 3)),
             dma((2, 4)),
             dma((2,)),
             dma((2,)),
@@ -828,33 +912,57 @@
     )(factor, adj)
 
 
-def merge_kernel(adj, panel, out):
+def merge_kernel(adj, panel, out, held, solved, sem):
     r, c = lax.axis_index("row"), lax.axis_index("col")
-    a = pl.program_id(0)
     shape = (256, 8, 128)
     slot = lax.broadcasted_iota(jnp.int32, (1, 8, 128), 1)
     lane = lax.broadcasted_iota(jnp.int32, (1, 8, 128), 2)
     col = (16 * (slot // 2) + c) * 256 + lax.rem(slot, 2) * 128 + lane
-    row = (8 * a + r) * 256 + lax.broadcasted_iota(jnp.int32, shape, 0)
-    value = jnp.where(row >= col, adj[...].reshape(shape), 0.0)
-    out[...] = value.reshape(2048, 128)
+    row = r * 256 + lax.broadcasted_iota(jnp.int32, shape, 0)
+
+    def rows(ref, a):
+        return ref.at[pl.ds(2048 * a, 2048)]
+
+    def come(a):
+        return pltpu.make_async_copy(rows(adj, a), held.at[a], sem.at[0, a])
+
+    def go(a):
+        return pltpu.make_async_copy(held.at[a], rows(out, a), sem.at[1, a])
+
+    fetch = pltpu.make_async_copy(panel, solved, sem.at[2, 0])
+    for a in range(8):
+        come(a).start()
 
     @pl.when(c < 2)
     def _():
-        for h in range(2):
-            out[pl.ds(h, 256, stride=8), :] = panel[pl.ds(h, 256, stride=2), :]
+        fetch.start()
+        fetch.wait()
+
+    for a in range(8):
+        come(a).wait()
+        held[a] = jnp.where(row + 2048 * a >= col, held[a].reshape(shape), 0.0).reshape(2048, 128)
+
+        @pl.when(c < 2)
+        def _():
+            for h in range(2):
+                held[a, pl.ds(h, 256, stride=8), :] = solved[pl.ds(512 * a + h, 256, stride=2), :]
+
+        go(a).start()
+    for a in range(8):
+        go(a).wait()
 
 
 def merge(adj, panel):
     return pl.pallas_call(
         merge_kernel,
-        grid=(8,),
         out_shape=jax.ShapeDtypeStruct((16384, 128), F32),
-        in_specs=[
-            pl.BlockSpec((2048, 128), lambda a: (a, 0)),
-            pl.BlockSpec((512, 128), lambda a: (a, 0)),
+        in_specs=[pl.BlockSpec(memory_space=pl.ANY)] * 2,
+        out_specs=pl.BlockSpec(memory_space=pl.ANY),
+        scratch_shapes=[
+            pltpu.VMEM((8, 2048, 128), F32),
+            pltpu.VMEM((4096, 128), F32),
+            pltpu.SemaphoreType.DMA((3, 8)),
         ],
-        out_specs=pl.BlockSpec((2048, 128), lambda a: (a, 0)),
         compiler_params=pltpu.CompilerParams(vmem_limit_bytes=60 * 2**20),
         name="merge",
     )(adj, panel)

time: 188 us -> 163 us (0.87)
  Pallas kernels: 188 us -> 163 us
    pallas_call x1, Pallas kernels: 178 us -> 155 us  [sweep(): pl.pallas_call(sweep_kernel, out_shape=jax.ShapeDtypeStruct((4096, 128),...]
where the time goes in v3:
time: 163 us
  Pallas kernels  163 us (100%)
    pallas_call x1, Pallas kernels, sweep(): pl.pallas_call(sweep_kernel, out_shape=jax.ShapeDtypeStruct((4096, 128),...  155 us
    pallas_call x1, Pallas kernels, merge(): pl.pallas_call(merge_kernel, out_shape=jax.ShapeDtypeStruct((16384, 128),...  7.77 us

profile of v3, /device:TPU:3, one launch (start us, length us, event | category | flops | bytes accessed | tf_op | source)
XLA Modules:
  0.0 163.4 jit_solution(6917467965720544679)
XLA Ops:
  0.0 155.4 %sweep.1.panel = f32[4096,128]{1,0:T(8,128)} custom-call(f32[16384,128]{1,0:T(8,128)} %bitcast.5, f32[16384,128]{1,0:T(8,128)} %bitcast.3), custom_call_target="tpu_custom_call" | custom-call | tf_op jit(solution)/shard_map/sweep/pallas_call | solution.py:848
  155.4 7.8 %merge.1 = f32[16384,128]{1,0:T(8,128)} custom-call(f32[16384,128]{1,0:T(8,128)} %bitcast.4, f32[4096,128]{1,0:T(8,128)} %sweep.1.panel), custom_call_target="tpu_custom_call" | custom-call | tf_op jit(solution)/shard_map/merge/pallas_call | solution.py:956

commit v4 on v3

--- a/solution.py
+++ b/solution.py
@@ -58,15 +58,24 @@
     return jnp.where(row > col, matrix, jnp.where(row == col, 0.5 * matrix, 0.0))
 
 
-def inverses(blocks):
+def inverse_open(blocks):
     row, col = iotas(blocks[0].shape)
-    found = [jnp.where(row == col, 1.0 / jnp.where(row == col, q, 1.0), 0.0) for q in blocks]
-    size = 1
-    while size < blocks[0].shape[0]:
+    pair = jnp.logical_and(row // 2 == col // 2, row > col)
+    found = []
+    for q in blocks:
+        diag = jnp.where(row == col, 1.0 / jnp.where(row == col, q, 1.0), 0.0)
+        down_rows = jnp.sum(diag, axis=1, keepdims=True)
+        down_cols = jnp.sum(diag, axis=0, keepdims=True)
+        found.append(diag - jnp.where(pair, down_rows * q * down_cols, 0.0))
+    return found
+
+
+def inverse_grow(found, blocks, sizes):
+    row, col = iotas(blocks[0].shape)
+    for size in sizes:
         here = jnp.logical_and(row // (2 * size) == col // (2 * size), row // size > col // size)
         left = [exact(x, jnp.where(here, q, 0.0)) for x, q in zip(found, blocks)]
         found = [x - exact(y, x) for x, y in zip(found, left)]
-        size *= 2
     return found
 
 
@@ -105,9 +114,11 @@
     nbr1,
     near,
     agath,
+    gstage,
     apiece,
     qbuf,
     qinv,
+    qwork,
     tpart,
     tin1,
     tsum,
@@ -135,6 +146,8 @@
     moved_sem,
     ga_s,
     ga_r,
+    gst_s,
+    gst_r,
     t1,
     t2,
     t3,
@@ -298,15 +311,17 @@
         post(held, held, ag2.at[0, w, p, q, 0], ag2.at[1, w, p, q, 0], member(p, f, up(s)))
         post(held, held, ag2.at[0, w, p, q, 1], ag2.at[1, w, p, q, 1], member(p, f, down(s)))
 
+    def scattered(w):
+        for p in range(2):
+
+            @pl.when(c != p)
+            def _():
+                arrived(wave(crow.at[p, c], w), scat_r.at[p, w])
+
     def gather_open(w):
         for p in range(2):
             f, s = place[p]
             held = wave(crow.at[p, piece(p, f, s)], w)
-
-            @pl.when(c != p)
-            def _():
-                arrived(wave(crow.at[p, c], w), scat_r.at[p, w])
-
             post(held, held, ag1.at[0, w, p, 0], ag1.at[1, w, p, 0], member(p, up(f), s))
             post(held, held, ag1.at[0, w, p, 1], ag1.at[1, w, p, 1], member(p, down(f), s))
             gather_second(p, w, 0, f)
@@ -402,13 +417,73 @@
         for n, t in ((5, y), (6, down(y)), (7, up(y)), (8, across_from(y))):
             arrived(ccol.at[t, 1 - core], col_sem.at[1, n])
 
+    def adjoint_block(a, b):
+        return jnp.concatenate(
+            [s_ref[pl.ds(a * 2048 + 2 * b + h, 256, stride=8), :] for h in range(2)], axis=1
+        )
+
+    row_iota, col_iota = iotas((256, 256))
+
+    def active(a, b):
+        i, j = 8 * a + r, 16 * b + c
+        return jnp.logical_and(j >= 2, j <= i)
+
+    macc[...] = jnp.zeros_like(macc)
+
+    def mirrored(a):
+        for p in range(2):
+            for half in range(2):
+                high, low = split(crow[p, 2 * a + half])
+                lanes = pl.ds(128 * half, 128)
+                ct[0, pl.ds(256 * p, 256), lanes] = high.T
+                ct[1, pl.ds(256 * p, 256), lanes] = low.T
+
+        def per_block(b, carry):
+            @pl.when(active(a, b))
+            def _():
+                total = dot3((ct[0], ct[1]), (sw[0, a, b], sw[1, a, b]))
+                macc[b, 0] += total[:, :128]
+                macc[b, 1] += total[:, 128:]
+
+            return carry
+
+        lax.fori_loop(0, 4, per_block, 0)
+
+    def prepare(a, carry):
+        def per_block(b, inner):
+            @pl.when(active(a, b))
+            def _():
+                shift = 256 * (8 * a + r - 16 * b - c)
+                block = jnp.where(row_iota + shift >= col_iota, adjoint_block(a, b), 0.0)
+                sw[0, a, b], sw[1, a, b] = split(block)
+
+            return inner
+
+        lax.fori_loop(0, 4, per_block, 0)
+        return carry
+
     for w in range(WAVES):
         pass_on(w)
+        scattered(w)
+        if w == WAVES - 1:
+            column_send()
         gather_open(w)
-    column_send()
     for w in range(WAVES):
         gather_first(w)
     column_open()
+    load.wait()
+
+    @pl.when(at_11)
+    def _():
+        rsend[...] = adjoint_block(0, 0)
+        send(rsend, rblk.at[0], blk_sem.at[0], blk_sem.at[2], (0, 0))
+
+    @pl.when(at_10)
+    def _():
+        rsend[...] = adjoint_block(0, 0)
+        send(rsend, rblk.at[1], blk_sem.at[1], blk_sem.at[3], (0, 0))
+
+    lax.fori_loop(0, 8, prepare, 0)
     for w in range(WAVES):
         gather_relay(w, 0)
         gather_relay(w, 1)
@@ -417,10 +492,12 @@
         gather_relay(w, 2)
         gather_relay(w, 3)
     column_close()
+
+    pair = lax.div(x, 2)
+    for owner in (z, up(z), down(z)):
+        mirrored(2 * owner + pair)
     for w in range(WAVES):
         gather_close(w)
-
-    load.wait()
 
     pivots = ((0, 0, 0), (1, 0, 1), (2, 1, 1))
 
@@ -437,55 +514,9 @@
             own.start()
             own.wait()
 
-    def adjoint_block(a, b):
-        return jnp.concatenate(
-            [s_ref[pl.ds(a * 2048 + 2 * b + h, 256, stride=8), :] for h in range(2)], axis=1
-        )
-
-    @pl.when(at_11)
-    def _():
-        rsend[...] = adjoint_block(0, 0)
-        send(rsend, rblk.at[0], blk_sem.at[0], blk_sem.at[2], (0, 0))
-
-    @pl.when(at_10)
-    def _():
-        rsend[...] = adjoint_block(0, 0)
-        send(rsend, rblk.at[1], blk_sem.at[1], blk_sem.at[3], (0, 0))
-
-    row_iota, col_iota = iotas((256, 256))
-
-    def active(a, b):
-        i, j = 8 * a + r, 16 * b + c
-        return jnp.logical_and(j >= 2, j <= i)
-
-    macc[...] = jnp.zeros_like(macc)
-
-    def mirrored(a):
-        for p in range(2):
-            for half in range(2):
-                high, low = split(crow[p, 2 * a + half])
-                lanes = pl.ds(128 * half, 128)
-                ct[0, pl.ds(256 * p, 256), lanes] = high.T
-                ct[1, pl.ds(256 * p, 256), lanes] = low.T
-
-        def per_block(b, carry):
-            @pl.when(active(a, b))
-            def _():
-                shift = 256 * (8 * a + r - 16 * b - c)
-                block = jnp.where(row_iota + shift >= col_iota, adjoint_block(a, b), 0.0)
-                high, low = split(block)
-                sw[0, a, b] = high
-                sw[1, a, b] = low
-                total = dot3((ct[0], ct[1]), (high, low))
-                macc[b, 0] += total[:, :128]
-                macc[b, 1] += total[:, 128:]
-
-            return carry
-
-        lax.fori_loop(0, 4, per_block, 0)
-
-    for step in range(8):
-        mirrored(step)
+    for step in range(4):
+        mirrored(2 * step + 1 - pair)
+    mirrored(2 * across_from(z) + pair)
 
     for b in range(4):
         post(
@@ -627,26 +658,37 @@
         mine[...] = mine[...] + mate_in[b]
     ring_open(*column_ring)
 
+    for slot, p, holder in pivots:
+
+        @pl.when(r != holder)
+        def _():
+            arrived(qbuf.at[slot], q_r.at[slot])
+
+            @pl.when(core == holder)
+            def _():
+                send(qbuf.at[slot], qbuf.at[slot], q_s.at[slot, 3], q_r.at[slot], mate)
+
+    def pivot(slot):
+        return jnp.concatenate([qbuf[slot, 0], qbuf[slot, 1]], axis=0)
+
+    def corners():
+        return [qbuf[slot, h, :, 128 * h : 128 * h + 128] for slot in (0, 2) for h in range(2)]
+
+    started = inverse_grow(inverse_open(corners()), corners(), (2, 4, 8))
+    for n in range(4):
+        qwork[n] = started[n]
+
     for spec in rings:
         ring_pass(*spec)
     ring_pass(*column_ring)
 
-    for slot, p, holder in pivots:
-
-        @pl.when(r != holder)
-        def _():
-            arrived(qbuf.at[slot], q_r.at[slot])
-
-            @pl.when(core == holder)
-            def _():
-                send(qbuf.at[slot], qbuf.at[slot], q_s.at[slot, 3], q_r.at[slot], mate)
-
-    def pivot(slot):
-        return jnp.concatenate([qbuf[slot, 0], qbuf[slot, 1]], axis=0)
-
-    inverse_0, inverse_1 = inverses([pivot(0), pivot(2)])
-    qinv[0] = inverse_0
-    qinv[1] = inverse_1
+    grown = inverse_grow([qwork[n] for n in range(4)], corners(), (16, 32, 64))
+    for n, slot in enumerate((0, 2)):
+        first, second = grown[2 * n : 2 * n + 2]
+        qinv[n, :128, :128] = first
+        qinv[n, :128, 128:] = jnp.zeros_like(first)
+        qinv[n, 128:, :128] = -exact(exact(second, qbuf[slot, 1, :, :128]), first)
+        qinv[n, 128:, 128:] = second
 
     for spec in rings:
         ring_close(*spec)
@@ -676,13 +718,38 @@
     solved_1 = times(sums_1, parts_1)
     apiece[1] = solved_1
 
+    def pick(table, default):
+        found = default
+        for k, value in table.items():
+            found = jnp.where(c == k, value, found)
+        return found
+
     def hand_in(p):
-        @pl.when(c != p)
+        via = pick({k: v for k, (v, _) in relays[p].items()}, -1)
+        slot = pick({k: n for k, (_, n) in relays[p].items()}, 0)
+
+        @pl.when(via >= 0)
+        def _():
+            send(apiece.at[p], gstage.at[slot], ga_s.at[p], gst_r.at[slot], (r, via))
+
+        @pl.when(jnp.logical_and(via < 0, c != p))
         def _():
             send(apiece.at[p], agath.at[c], ga_s.at[p], ga_r.at[c], (r, p))
 
+    def hand_on():
+        for p in range(2):
+            for via, members in groups[p].items():
+
+                @pl.when(c == via)
+                def _():
+                    for slot, k in enumerate(members):
+                        arrived(gstage.at[slot], gst_r.at[slot])
+                        send(gstage.at[slot], agath.at[k], gst_s.at[slot], ga_r.at[k], (r, p))
+
+    hand_in(1)
     solved_0 = times(sums_0 - times(solved_1, pivot(1)), parts_0)
     apiece[0] = solved_0
+    hand_in(0)
 
     sides_1, sides_0 = [tuple(v.T for v in split(m)) for m in (solved_1, solved_0)]
     right_1, right_0 = split(crow[1, c]), split(crow[0, c])
@@ -692,8 +759,6 @@
     for step in range(1, 8):
         to = lax.rem(r + step, 8)
         post(tpart.at[to], tin1.at[step], t1.at[0, step], t1.at[1, step], (to, c))
-    hand_in(1)
-    hand_in(0)
     result = tpart[r]
     for step in range(1, 8):
         arrived(tin1.at[step], t1.at[1, step])
@@ -725,6 +790,8 @@
         def _():
             send(tslice, tall.at[r, x], t3.at[0], troot.at[r, x], (0, 0))
 
+    hand_on()
+
     def flat(parts):
         return jnp.concatenate(parts, axis=0)
 
@@ -809,6 +876,7 @@
             def _():
                 for w in range(WAVES):
                     left(stage.at[slot, w], stage_s.at[slot, w])
+                left(gstage.at[slot], gst_s.at[slot])
 
     @pl.when(from_away)
     def _():
@@ -869,9 +937,11 @@
             vmem((2, 4, 2, 128, 256), F32),
             vmem((2, 3, 128, 256), F32),
             vmem((16, 128, 256), F32),
+            vmem((4, 128, 256), F32),
             vmem((2, 128, 256), F32),
             vmem((3, 2, 128, 256), F32),
             vmem((2, 256, 256), F32),
+            vmem((4, 128, 128), F32),
             vmem((8, 3, 32, 256), F32),
             vmem((8, 3, 32, 256), F32),
             vmem((4, 3, 8, 256), F32),
@@ -899,6 +969,8 @@
             dma((2,)),
             dma((2,)),
             dma((16,)),
+            dma((4,)),
+            dma((4,)),
             dma((2, 8)),
             dma((2, 4)),
             dma((4,)),

time: 163 us -> 150 us (0.920)
  Pallas kernels: 163 us -> 149 us
    pallas_call x1, Pallas kernels: 155 us -> 142 us  [sweep(): pl.pallas_call(sweep_kernel, out_shape=jax.ShapeDtypeStruct((4096, 128),...]
where the time goes in v4:
time: 150 us
  Pallas kernels  149 us (99%)
    pallas_call x1, Pallas kernels, sweep(): pl.pallas_call(sweep_kernel, out_shape=jax.ShapeDtypeStruct((4096, 128),...  142 us
    pallas_call x1, Pallas kernels, merge(): pl.pallas_call(merge_kernel, out_shape=jax.ShapeDtypeStruct((16384, 128),...  7.77 us

profile of v4, /device:TPU:3, one launch (start us, length us, event | category | flops | bytes accessed | tf_op | source)
XLA Modules:
  0.0 149.6 jit_solution(17053489789130001013)
XLA Ops:
  0.0 141.6 %sweep.1.panel = f32[4096,128]{1,0:T(8,128)} custom-call(f32[16384,128]{1,0:T(8,128)} %bitcast.5, f32[16384,128]{1,0:T(8,128)} %bitcast.3), custom_call_target="tpu_custom_call" | custom-call | tf_op jit(solution)/shard_map/sweep/pallas_call | solution.py:916
  141.7 7.8 %merge.1 = f32[16384,128]{1,0:T(8,128)} custom-call(f32[16384,128]{1,0:T(8,128)} %bitcast.4, f32[4096,128]{1,0:T(8,128)} %sweep.1.panel), custom_call_target="tpu_custom_call" | custom-call | tf_op jit(solution)/shard_map/merge/pallas_call | solution.py:1028

commit v5 on v4

--- a/solution.py
+++ b/solution.py
@@ -80,7 +80,12 @@
 
 
 def times(left, right):
-    return dot3(left if isinstance(left, tuple) else split(left), right if isinstance(right, tuple) else split(right))
+    left_high, left_low = left if isinstance(left, tuple) else split(left)
+    right_high, right_low = right if isinstance(right, tuple) else split(right)
+    return dot(
+        jnp.concatenate([left_low, left_high, left_high], axis=1),
+        jnp.concatenate([right_high, right_low, right_high], axis=0),
+    )
 
 
 def turned(parts):
@@ -193,19 +198,37 @@
         ).wait_send()
 
     holds_panel = c < 2
+
+    def factor_part(n):
+        part = pl.ds(4096 * n, 4096)
+        return pltpu.make_async_copy(factor.at[part], s_ref.at[part], local_sem.at[2 + n])
+
     load = pltpu.make_async_copy(adj, s_ref, local_sem.at[0])
 
     @pl.when(holds_panel)
     def _():
-        pltpu.make_async_copy(factor, s_ref, local_sem.at[1]).start()
+        for n in range(4):
+            factor_part(n).start()
 
     barrier = pltpu.get_barrier_semaphore()
 
     def greet(device):
         pl.semaphore_signal(barrier, inc=1, device_id=device, device_id_type=MESH)
 
-    for step in range(1, 16):
-        greet((r, lax.rem(c + step, 16)))
+    for step in range(1, 4):
+        greet((r, 4 * z + lax.rem(x + step, 4)))
+        greet((r, 4 * lax.rem(z + step, 4) + x))
+    diagonal = ((4, 9), (12, 10), (12, 11), (5, 8), (13, 11), (13, 10))
+    for one, other in diagonal:
+
+        @pl.when(c == one)
+        def _():
+            greet((r, other))
+
+        @pl.when(c == other)
+        def _():
+            greet((r, one))
+
     for step in range(1, 8):
         greet((lax.rem(r + step, 8), c))
     away = jnp.logical_or(target[0] != r, target[1] != c)
@@ -235,19 +258,20 @@
 
     @pl.when(holds_panel)
     def _():
-        pltpu.make_async_copy(factor, s_ref, local_sem.at[1]).wait()
-
         def take(k, carry):
             for h in range(2):
                 panel[k, :, pl.ds(128 * h, 128)] = s_ref[pl.ds(k * 1024 + h, 128, stride=8), :]
             return carry
 
-        lax.fori_loop(0, 16, take, 0)
+        for n in range(4):
+            factor_part(n).wait()
+            lax.fori_loop(4 * n, 4 * n + 4, take, 0)
 
     load.start()
     pl.semaphore_wait(
         barrier,
-        22
+        13
+        + sum(jnp.where(jnp.logical_or(c == one, c == other), 1, 0) for one, other in diagonal)
         + jnp.where(away, 1, 0)
         + jnp.where(from_away, 1, 0)
         + jnp.where(owes_root, 1, 0)
@@ -736,15 +760,14 @@
         def _():
             send(apiece.at[p], agath.at[c], ga_s.at[p], ga_r.at[c], (r, p))
 
-    def hand_on():
-        for p in range(2):
-            for via, members in groups[p].items():
-
-                @pl.when(c == via)
-                def _():
-                    for slot, k in enumerate(members):
-                        arrived(gstage.at[slot], gst_r.at[slot])
-                        send(gstage.at[slot], agath.at[k], gst_s.at[slot], ga_r.at[k], (r, p))
+    def hand_on(p):
+        for via, members in groups[p].items():
+
+            @pl.when(c == via)
+            def _():
+                for slot, k in enumerate(members):
+                    arrived(gstage.at[slot], gst_r.at[slot])
+                    send(gstage.at[slot], agath.at[k], gst_s.at[slot], ga_r.at[k], (r, p))
 
     hand_in(1)
     solved_0 = times(sums_0 - times(solved_1, pivot(1)), parts_0)
@@ -759,6 +782,7 @@
     for step in range(1, 8):
         to = lax.rem(r + step, 8)
         post(tpart.at[to], tin1.at[step], t1.at[0, step], t1.at[1, step], (to, c))
+    hand_on(1)
     result = tpart[r]
     for step in range(1, 8):
         arrived(tin1.at[step], t1.at[1, step])
@@ -790,7 +814,7 @@
         def _():
             send(tslice, tall.at[r, x], t3.at[0], troot.at[r, x], (0, 0))
 
-    hand_on()
+    hand_on(0)
 
     def flat(parts):
         return jnp.concatenate(parts, axis=0)
@@ -800,7 +824,7 @@
         tall[0, 0] = tslice[...]
         link = split(pivot(1))
         pivot_1, pivot_0 = turned(split(pivot(2))), turned(split(pivot(0)))
-        ahead = split(times(link, parts_0))
+        ahead = turned(split(times(link, parts_0)))
         for t in range(8):
             for n in range(4):
                 if t + n > 0:
@@ -814,11 +838,12 @@
         diag_1 = diag_step(pivot_1, parts_1, lower(rblk[0] - total(0)))
         rblk[0] = diag_1
         send(rblk.at[0], a01, blk_sem.at[6], blk_sem.at[5], (1, 1))
-        rows_1 = times(rblk[1] - total(1), parts_0) - times(diag_1 + diag_1.T, ahead)
-        rsend[...] = rows_1
+        known = times(rblk[1] - total(1), parts_0)
+        rest = lower(adjoint_block(0, 0) - total(2) - times(turned(split(known)), link))
+        linked = split(times(diag_1 + diag_1.T, link))
+        rsend[...] = known - times(linked, parts_0)
         send(rsend, a01, blk_sem.at[4], blk_sem.at[5], (1, 0))
-        sums = total(2) + times(turned(split(rows_1)), link)
-        done[...] = diag_step(pivot_0, parts_0, lower(adjoint_block(0, 0) - sums))
+        done[...] = diag_step(pivot_0, parts_0, rest + lower(times(ahead, linked)))
         left(rsend, blk_sem.at[4])
         left(rblk.at[0], blk_sem.at[6])
 

time: 150 us -> 148 us (0.987)
  no operation moved by 1% of the time
where the time goes in v5:
time: 148 us
  Pallas kernels  148 us (100%)
    pallas_call x1, Pallas kernels, sweep(): pl.pallas_call(sweep_kernel, out_shape=jax.ShapeDtypeStruct((4096, 128),...  140 us
    pallas_call x1, Pallas kernels, merge(): pl.pallas_call(merge_kernel, out_shape=jax.ShapeDtypeStruct((16384, 128),...  7.77 us

profile of v5, /device:TPU:3, one launch (start us, length us, event | category | flops | bytes accessed | tf_op | source)
XLA Modules:
  0.0 148.2 jit_solution(8420960308074187901)
XLA Ops:
  0.0 140.3 %sweep.1.panel = f32[4096,128]{1,0:T(8,128)} custom-call(f32[16384,128]{1,0:T(8,128)} %bitcast.5, f32[16384,128]{1,0:T(8,128)} %bitcast.3), custom_call_target="tpu_custom_call" | custom-call | tf_op jit(solution)/shard_map/sweep/pallas_call | solution.py:941
  140.3 7.8 %merge.1 = f32[16384,128]{1,0:T(8,128)} custom-call(f32[16384,128]{1,0:T(8,128)} %bitcast.4, f32[4096,128]{1,0:T(8,128)} %sweep.1.panel), custom_call_target="tpu_custom_call" | custom-call | tf_op jit(solution)/shard_map/merge/pallas_call | solution.py:1053
